TPU v7x, 128 devices: a whole 4x4x4 slice. The times are simulated.
128 devices in a mesh: dp: 4 (over y), ctx: 32 (over z, x, core).
Axes of the slice: x: 4, y: 4, z: 4, core: 2. Of those that a mesh axis runs over, the one named last changes fastest.
Arguments:
- queries: bfloat16 [16384, 64, 128], P(('dp', 'ctx')), parts along dimension 0, may hold values from -6 to 6
- keys: bfloat16 [16384, 8, 128], P(('dp', 'ctx')), parts along dimension 0, may hold values from -6 to 6
- values: bfloat16 [16384, 8, 128], P(('dp', 'ctx')), parts along dimension 0, may hold values from -6 to 6
- output: bfloat16 [16384, 64, 128], P(('dp', 'ctx')), parts along dimension 0, may hold values from -6 to 6
- output_cotangent: bfloat16 [16384, 64, 128], P(('dp', 'ctx')), parts along dimension 0, may hold values from -6 to 6
- logsumexp_rows: float32 [16384, 64], P(('dp', 'ctx')), parts along dimension 0, may hold values from 2 to 4
- doc_lengths: int32 [64], P('dp'), parts along dimension 0, may hold values from 1 to 512, 4096 in all
Outputs:
- query_grad: bfloat16 [16384, 64, 128], P(('dp', 'ctx')), parts along dimension 0
- key_grad: bfloat16 [16384, 8, 128], P(('dp', 'ctx')), parts along dimension 0
- value_grad: bfloat16 [16384, 8, 128], P(('dp', 'ctx')), parts along dimension 0
There are 4 independent parts, one for each index of `dp`. A program takes and returns all parts, laid end to end along the dimension named above; each array names one. Nothing has to cross between parts.
Inputs may be any that keep to these rules, and one draw needn't show every extreme that they name: `doc_lengths`: the 16 lengths sum to 4096; the largest is exactly 512.
All inputs are finite; a program needn't handle non-finite values.
Results may differ from a plain program's by a relative error of at most 0.0057.
Values may be sent and summed in bfloat16 or wider, within the bound.
No kernel may reach another device: no remote copies, remote signals or barrier semaphores. Data moves between devices by JAX's collectives and lax.ppermute only.
A program may use at most 128 MiB of HBM per device.

v0:
```python
import jax
import jax.numpy as jnp
from jax import lax
from jax.sharding import PartitionSpec as P

BLOCK = 512
DOC_MAX = 512


def document_ids(doc_lengths, grand_total):
    ends = jnp.cumsum(doc_lengths)
    positions = jnp.arange(grand_total, dtype=jnp.int32)
    return jnp.sum((positions[:, None] >= ends[None, :]).astype(jnp.int32), axis=1)


def group_grads(
    queries, output_cotangent, logsumexp_rows, output_dot_grad, keys, values, doc_id, block, doc_max
):
    grand_total, heads, width = queries.shape
    scale = width ** (-0.5)
    window = doc_max + block
    key_pad = jnp.concatenate([jnp.zeros((doc_max, width), keys.dtype), keys], 0)
    value_pad = jnp.concatenate([jnp.zeros((doc_max, width), values.dtype), values], 0)
    id_pad = jnp.concatenate([jnp.full((doc_max,), -1, jnp.int32), doc_id], 0)

    def step(carry, index):
        key_acc, value_acc = carry
        start = index * block
        q_blk = lax.dynamic_slice_in_dim(queries, start, block, 0)
        g_blk = lax.dynamic_slice_in_dim(output_cotangent, start, block, 0)
        lse_blk = lax.dynamic_slice_in_dim(logsumexp_rows, start, block, 0)
        del_blk = lax.dynamic_slice_in_dim(output_dot_grad, start, block, 0)
        k_win = lax.dynamic_slice_in_dim(key_pad, start, window, 0)
        v_win = lax.dynamic_slice_in_dim(value_pad, start, window, 0)
        id_q = lax.dynamic_slice_in_dim(doc_id, start, block, 0)
        id_k = lax.dynamic_slice_in_dim(id_pad, start, window, 0)
        q_pos = start + jnp.arange(block, dtype=jnp.int32)
        k_pos = start - doc_max + jnp.arange(window, dtype=jnp.int32)
        visible = (id_q[:, None] == id_k[None, :]) & (k_pos[None, :] <= q_pos[:, None])
        score = jnp.einsum("qhd,kd->hqk", q_blk, k_win, preferred_element_type=jnp.float32) * scale
        prob = jnp.where(visible[None], jnp.exp(score - lse_blk.T[:, :, None]), 0.0)
        prob_b = prob.astype(jnp.bfloat16)
        value_part = jnp.einsum("hqk,qhd->kd", prob_b, g_blk, preferred_element_type=jnp.float32)
        dprob = jnp.einsum("qhd,kd->hqk", g_blk, v_win, preferred_element_type=jnp.float32)
        dscore = (prob * (dprob - del_blk.T[:, :, None])).astype(jnp.bfloat16)
        q_grad = (
            jnp.einsum("hqk,kd->qhd", dscore, k_win, preferred_element_type=jnp.float32) * scale
        ).astype(jnp.bfloat16)
        key_part = (
            jnp.einsum("hqk,qhd->kd", dscore, q_blk, preferred_element_type=jnp.float32) * scale
        )
        key_acc = lax.dynamic_update_slice_in_dim(
            key_acc, lax.dynamic_slice_in_dim(key_acc, start, window, 0) + key_part, start, 0
        )
        value_acc = lax.dynamic_update_slice_in_dim(
            value_acc, lax.dynamic_slice_in_dim(value_acc, start, window, 0) + value_part, start, 0
        )
        return ((key_acc, value_acc), q_grad)

    zeros = jnp.zeros((doc_max + grand_total, width), jnp.float32)
    (key_acc, value_acc), q_grads = lax.scan(
        step, (zeros, zeros), jnp.arange(grand_total // block, dtype=jnp.int32)
    )
    return (q_grads.reshape(grand_total, heads, width), key_acc[doc_max:], value_acc[doc_max:])


def per_device(queries, keys, values, output, output_cotangent, logsumexp_rows, doc_lengths):
    count = lax.axis_size("ctx")
    tok_rows = queries.shape[0]
    kv_heads = keys.shape[1]
    width = keys.shape[2]
    grand_total = tok_rows * count
    doc_id = document_ids(doc_lengths, grand_total)
    group = count * kv_heads // queries.shape[1]
    got_q, got_g, got_o = (
        lax.all_to_all(queries, "ctx", split_axis=1, concat_axis=0, tiled=True),
        lax.all_to_all(output_cotangent, "ctx", split_axis=1, concat_axis=0, tiled=True),
        lax.all_to_all(output, "ctx", split_axis=1, concat_axis=0, tiled=True),
    )
    got_lse = lax.all_to_all(logsumexp_rows, "ctx", split_axis=1, concat_axis=0, tiled=True)
    got_delta = jnp.sum(got_g.astype(jnp.float32) * got_o.astype(jnp.float32), axis=-1)
    key_slots = jnp.repeat(keys, group, axis=1)
    value_slots = jnp.repeat(values, group, axis=1)
    key_recv, value_recv = (
        lax.all_to_all(key_slots, "ctx", split_axis=1, concat_axis=0, tiled=True),
        lax.all_to_all(value_slots, "ctx", split_axis=1, concat_axis=0, tiled=True),
    )
    key_full = key_recv[:, 0]
    value_full = value_recv[:, 0]
    q_grad, k_grad, v_grad = group_grads(
        got_q, got_g, got_lse, got_delta, key_full, value_full, doc_id, BLOCK, DOC_MAX
    )
    query_grad = lax.all_to_all(q_grad, "ctx", split_axis=0, concat_axis=1, tiled=True)
    key_back, value_back = (
        lax.all_to_all(k_grad[:, None], "ctx", split_axis=0, concat_axis=1, tiled=True),
        lax.all_to_all(v_grad[:, None], "ctx", split_axis=0, concat_axis=1, tiled=True),
    )
    key_grad = jnp.sum(key_back.reshape(tok_rows, kv_heads, group, width), axis=2).astype(
        jnp.bfloat16
    )
    value_grad = jnp.sum(value_back.reshape(tok_rows, kv_heads, group, width), axis=2).astype(
        jnp.bfloat16
    )
    return (query_grad, key_grad, value_grad)


def solution(mesh):
    in_specs = (
        P(("dp", "ctx"), None, None),
        P(("dp", "ctx"), None, None),
        P(("dp", "ctx"), None, None),
        P(("dp", "ctx"), None, None),
        P(("dp", "ctx"), None, None),
        P(("dp", "ctx"), None),
        P("dp"),
    )
    out_specs = (
        P(("dp", "ctx"), None, None),
        P(("dp", "ctx"), None, None),
        P(("dp", "ctx"), None, None),
    )
    return jax.shard_map(
        per_device, mesh=mesh, in_specs=in_specs, out_specs=out_specs, check_vma=False
    )
```

profile of v0, /device:TPU:55, one launch (start us, length us, event | category | flops | bytes accessed | tf_op | source)
XLA Modules:
  0.0 433.7 jit_solution(12046688011223629000)
XLA Ops:
  2.9 8.3 %all-to-all-start = ((bf16[128,32,128]{2,0,1:T(8,128)(2,1)}), bf16[128,32,128]{2,0,1:T(8,128)(2,1)S(1)}, u32[]{:S(2)}, u32[]{:S(2)}) async-start(bf16[128,32,128]{2,0,1:T(8,128)(2,1)} %bitcast.13), calls=%async_computation | async-start | bytes 2097152 | tf_op jit(solution)/shard_map/all_to_all | solution.py:85
  11.2 15.0 %all-to-all-done = bf16[128,32,128]{2,0,1:T(8,128)(2,1)S(1)} async-done(((bf16[128,32,128]{2,0,1:T(8,128)(2,1)}), bf16[128,32,128]{2,0,1:T(8,128)(2,1)S(1)}, u32[]{:S(2)}, u32[]{:S(2)}) %all-to-all-start) | async-done | bytes 1048608 | tf_op jit(solution)/shard_map/all_to_all | solution.py:85
  27.4 6.2 %all-to-all-start.3 = ((bf16[128,32,128]{2,0,1:T(8,128)(2,1)}), bf16[128,32,128]{2,0,1:T(8,128)(2,1)S(1)}, u32[]{:S(2)}, u32[]{:S(2)}) async-start(bf16[128,32,128]{2,0,1:T(8,128)(2,1)} %bitcast.23), calls=%async_computation.3 | async-start | bytes 2097152 | tf_op jit(solution)/shard_map/all_to_all | solution.py:86
  33.6 4.3 copy.82
  37.9 10.8 %all-to-all-done.3 = bf16[128,32,128]{2,0,1:T(8,128)(2,1)S(1)} async-done(((bf16[128,32,128]{2,0,1:T(8,128)(2,1)}), bf16[128,32,128]{2,0,1:T(8,128)(2,1)S(1)}, u32[]{:S(2)}, u32[]{:S(2)}) %all-to-all-start.3) | async-done | bytes 1048608 | tf_op jit(solution)/shard_map/all_to_all | solution.py:86
  49.7 6.3 %all-to-all-start.4 = ((bf16[128,64,128]{2,0,1:T(8,128)(2,1)}), bf16[128,64,128]{2,0,1:T(8,128)(2,1)S(1)}, u32[]{:S(2)}, u32[]{:S(2)}) async-start(bf16[128,64,128]{2,0,1:T(8,128)(2,1)} %copy.82), calls=%async_computation.4 | async-start | bytes 4194304 | tf_op jit(solution)/shard_map/all_to_all | solution.py:77
  56.0 4.3 copy.84
  60.3 22.9 %all-to-all-done.4 = bf16[128,64,128]{2,0,1:T(8,128)(2,1)S(1)} async-done(((bf16[128,64,128]{2,0,1:T(8,128)(2,1)}), bf16[128,64,128]{2,0,1:T(8,128)(2,1)S(1)}, u32[]{:S(2)}, u32[]{:S(2)}) %all-to-all-start.4) | async-done | bytes 2097184 | tf_op jit(solution)/shard_map/all_to_all | solution.py:77
  83.1 7.5 %all-to-all-start.5 = ((bf16[128,64,128]{2,0,1:T(8,128)(2,1)}), bf16[128,64,128]{2,0,1:T(8,128)(2,1)}, u32[]{:S(2)}, u32[]{:S(2)}) async-start(bf16[128,64,128]{2,0,1:T(8,128)(2,1)} %copy.84), calls=%async_computation.5 | async-start | bytes 4194304 | tf_op jit(solution)/shard_map/all_to_all | solution.py:78
  90.6 4.3 copy.79
  94.9 22.9 %all-to-all-done.5 = bf16[128,64,128]{2,0,1:T(8,128)(2,1)} async-done(((bf16[128,64,128]{2,0,1:T(8,128)(2,1)}), bf16[128,64,128]{2,0,1:T(8,128)(2,1)}, u32[]{:S(2)}, u32[]{:S(2)}) %all-to-all-start.5) | async-done | bytes 2097184 | tf_op jit(solution)/shard_map/all_to_all | solution.py:78
  117.8 7.5 %all-to-all-start.1 = ((bf16[128,64,128]{2,0,1:T(8,128)(2,1)}), bf16[128,64,128]{2,0,1:T(8,128)(2,1)}, u32[]{:S(2)}, u32[]{:S(2)}) async-start(bf16[128,64,128]{2,0,1:T(8,128)(2,1)} %copy.79), calls=%async_computation.1 | async-start | bytes 4194304 | tf_op jit(solution)/shard_map/all_to_all | solution.py:76
  128.1 24.5 %all-to-all-done.1 = bf16[128,64,128]{2,0,1:T(8,128)(2,1)} async-done(((bf16[128,64,128]{2,0,1:T(8,128)(2,1)}), bf16[128,64,128]{2,0,1:T(8,128)(2,1)}, u32[]{:S(2)}, u32[]{:S(2)}) %all-to-all-start.1) | async-done | bytes 2097184 | tf_op jit(solution)/shard_map/all_to_all | solution.py:76
  152.6 6.7 %all-to-all-start.2 = ((f32[128,32,2]{0,2,1:T(2,128)}), f32[128,32,2]{0,2,1:T(2,128)S(1)}, u32[]{:S(2)}, u32[]{:S(2)}) async-start(f32[128,32,2]{0,2,1:T(2,128)} %bitcast.20), calls=%async_computation.2 | async-start | bytes 65536 | tf_op jit(solution)/shard_map/all_to_all | solution.py:80
  163.5 3.2 copy.80
  170.0 151.7 %while.16 = (s32[]{:T(128)}, f32[4608,128]{1,0:T(8,128)}, f32[4608,128]{1,0:T(8,128)}, bf16[8,512,2,128]{3,1,0,2:T(8,128)(2,1)}, s32[8]{0:T(128)S(1)}, /*index=5...) while((s32[]{:T(128)}, f32[4608,128]{1,0:T(8,128)}, ...), condition=%wide.region_4.5_spmd, body=%wide.region_3.4_spmd.sunk | while | flops 1354892800 | bytes 25750340 | solution.py:61
  171.2 3.7 fusion.69
  175.9 3.7 fusion.70
  184.6 4.3 fusion.72
  190.2 3.7 fusion.69
  194.9 3.7 fusion.70
  203.6 4.3 fusion.72
  209.1 3.7 fusion.69
  213.8 3.7 fusion.70
  222.5 4.3 fusion.72
  228.1 3.7 fusion.69
  232.8 3.7 fusion.70
  241.5 4.3 fusion.72
  247.0 3.7 fusion.69
  251.7 3.7 fusion.70
  260.4 4.3 fusion.72
  266.0 3.7 fusion.69
  270.7 3.7 fusion.70
  279.4 4.3 %fusion.72 = f32[4608,128]{1,0:T(8,128)} fusion(f32[4608,128]{1,0:T(8,128)} %get-tuple-element.313, s32[]{:T(128)S(6)} %select_n.47, f32[1024,512,2]{1,0,2:T(8,128)} %fusion.69, f32[2,512]{1,0:T(2,128)S(1)} %get-tuple-element.291, pred[512,1024]{0,1:T(8,128)(4,1)S(1)} %compare_and_fusion.2, bf16[4096,2,128]{2,0,1:T(8,128)(2,1)} %get-tuple-element.341, ...), kind=kOutput, calls=%fused_computation.17.clone.1 | convolution fusion | flops 272760832 | bytes 6033416 | tf_op jit(solution)/shard_map/while/body/eval_jaxpr/hqk,qhd->kd/dot_general | solution.py:43
  284.9 3.7 fusion.69
  289.6 3.7 fusion.70
  298.3 4.4 %fusion.72 = f32[4608,128]{1,0:T(8,128)} fusion(f32[4608,128]{1,0:T(8,128)} %get-tuple-element.313, s32[]{:T(128)S(6)} %select_n.47, f32[1024,512,2]{1,0,2:T(8,128)} %fusion.69, f32[2,512]{1,0:T(2,128)S(1)} %get-tuple-element.291, pred[512,1024]{0,1:T(8,128)(4,1)S(1)} %compare_and_fusion.2, bf16[4096,2,128]{2,0,1:T(8,128)(2,1)} %get-tuple-element.341, ...), kind=kOutput, calls=%fused_computation.17.clone.1 | convolution fusion | flops 272760832 | bytes 6033416 | tf_op jit(solution)/shard_map/while/body/eval_jaxpr/hqk,qhd->kd/dot_general | solution.py:43
  303.9 3.7 fusion.69
  308.6 3.7 fusion.70
  317.4 4.3 %fusion.72 = f32[4608,128]{1,0:T(8,128)} fusion(f32[4608,128]{1,0:T(8,128)} %get-tuple-element.313, s32[]{:T(128)S(6)} %select_n.47, f32[1024,512,2]{1,0,2:T(8,128)} %fusion.69, f32[2,512]{1,0:T(2,128)S(1)} %get-tuple-element.291, pred[512,1024]{0,1:T(8,128)(4,1)S(1)} %compare_and_fusion.2, bf16[4096,2,128]{2,0,1:T(8,128)(2,1)} %get-tuple-element.341, ...), kind=kOutput, calls=%fused_computation.17.clone.1 | convolution fusion | flops 272760832 | bytes 6033416 | tf_op jit(solution)/shard_map/while/body/eval_jaxpr/hqk,qhd->kd/dot_general | solution.py:43
  321.7 5.8 %copy.86 = bf16[4096,2,128]{2,1,0:T(2,128)(2,1)} copy(bf16[4096,2,128]{2,0,1:T(8,128)(2,1)} %bitcast.144) | data formatting | bytes 4194304 | tf_op jit(solution)/shard_map/reshape | solution.py:64
  327.5 7.6 %all-to-all-start.6 = ((bf16[4096,2,128]{2,1,0:T(2,128)(2,1)}), bf16[4096,2,128]{2,1,0:T(2,128)(2,1)}, u32[]{:S(2)}, u32[]{:S(2)}) async-start(bf16[4096,2,128]{2,1,0:T(2,128)(2,1)} %copy.86), calls=%async_computation.6 | async-start | bytes 4194304 | tf_op jit(solution)/shard_map/all_to_all | solution.py:93
  336.5 25.7 %all-to-all-done.6 = bf16[4096,2,128]{2,1,0:T(2,128)(2,1)} async-done(((bf16[4096,2,128]{2,1,0:T(2,128)(2,1)}), bf16[4096,2,128]{2,1,0:T(2,128)(2,1)}, u32[]{:S(2)}, u32[]{:S(2)}) %all-to-all-start.6) | async-done | bytes 2097184 | tf_op jit(solution)/shard_map/all_to_all | solution.py:93
  362.2 6.9 %all-to-all-start.7 = ((f32[4096,1,128]{2,1,0:T(1,128)}), f32[4096,1,128]{2,1,0:T(1,128)S(1)}, u32[]{:S(2)}, u32[]{:S(2)}) async-start(f32[4096,1,128]{2,1,0:T(1,128)} %bitcast.138), calls=%async_computation.7 | async-start | bytes 4194304 | tf_op jit(solution)/shard_map/all_to_all | solution.py:95
  369.1 3.0 slice.7
  372.1 24.1 %all-to-all-done.7 = f32[4096,1,128]{2,1,0:T(1,128)S(1)} async-done(((f32[4096,1,128]{2,1,0:T(1,128)}), f32[4096,1,128]{2,1,0:T(1,128)S(1)}, u32[]{:S(2)}, u32[]{:S(2)}) %all-to-all-start.7) | async-done | bytes 2097184 | tf_op jit(solution)/shard_map/all_to_all | solution.py:95
  396.3 7.5 %all-to-all-start.8 = ((f32[4096,1,128]{2,1,0:T(1,128)}), f32[4096,1,128]{2,1,0:T(1,128)}, u32[]{:S(2)}, u32[]{:S(2)}) async-start(f32[4096,1,128]{2,1,0:T(1,128)} %bitcast.137), calls=%async_computation.8 | async-start | bytes 4194304 | tf_op jit(solution)/shard_map/all_to_all | solution.py:96
  409.6 21.4 %all-to-all-done.8 = f32[4096,1,128]{2,1,0:T(1,128)} async-done(((f32[4096,1,128]{2,1,0:T(1,128)}), f32[4096,1,128]{2,1,0:T(1,128)}, u32[]{:S(2)}, u32[]{:S(2)}) %all-to-all-start.8) | async-done | bytes 2097184 | tf_op jit(solution)/shard_map/all_to_all | solution.py:96
  (124 shorter events, 76.7 us)
Async XLA Ops:
  0.6 10.5 %copy-start.3 = (bf16[128,8,128]{2,1,0:T(8,128)(2,1)S(1)}, bf16[128,8,128]{2,1,0:T(8,128)(2,1)}, u32[]{:S(2)}) copy-start(bf16[128,8,128]{2,1,0:T(8,128)(2,1)} %param.11) | copy-start | bytes 786436
  2.9 23.3 %all-to-all-start = ((bf16[128,32,128]{2,0,1:T(8,128)(2,1)}), bf16[128,32,128]{2,0,1:T(8,128)(2,1)S(1)}, u32[]{:S(2)}, u32[]{:S(2)}) async-start(bf16[128,32,128]{2,0,1:T(8,128)(2,1)} %bitcast.13), calls=%async_computation | async-start | bytes 2097152 | tf_op jit(solution)/shard_map/all_to_all | solution.py:85
  27.4 21.3 %all-to-all-start.3 = ((bf16[128,32,128]{2,0,1:T(8,128)(2,1)}), bf16[128,32,128]{2,0,1:T(8,128)(2,1)S(1)}, u32[]{:S(2)}, u32[]{:S(2)}) async-start(bf16[128,32,128]{2,0,1:T(8,128)(2,1)} %bitcast.23), calls=%async_computation.3 | async-start | bytes 2097152 | tf_op jit(solution)/shard_map/all_to_all | solution.py:86
  48.7 1.0 copy-start.1
  49.7 33.5 %all-to-all-start.4 = ((bf16[128,64,128]{2,0,1:T(8,128)(2,1)}), bf16[128,64,128]{2,0,1:T(8,128)(2,1)S(1)}, u32[]{:S(2)}, u32[]{:S(2)}) async-start(bf16[128,64,128]{2,0,1:T(8,128)(2,1)} %copy.82), calls=%async_computation.4 | async-start | bytes 4194304 | tf_op jit(solution)/shard_map/all_to_all | solution.py:77
  83.1 34.7 %all-to-all-start.5 = ((bf16[128,64,128]{2,0,1:T(8,128)(2,1)}), bf16[128,64,128]{2,0,1:T(8,128)(2,1)}, u32[]{:S(2)}, u32[]{:S(2)}) async-start(bf16[128,64,128]{2,0,1:T(8,128)(2,1)} %copy.84), calls=%async_computation.5 | async-start | bytes 4194304 | tf_op jit(solution)/shard_map/all_to_all | solution.py:78
  94.9 30.5 %copy-start.4 = (s32[16]{0:T(128)S(1)}, s32[16]{0:T(128)}, u32[]{:S(2)}) copy-start(s32[16]{0:T(128)} %param.15) | copy-start | bytes 196
  117.8 34.7 %all-to-all-start.1 = ((bf16[128,64,128]{2,0,1:T(8,128)(2,1)}), bf16[128,64,128]{2,0,1:T(8,128)(2,1)}, u32[]{:S(2)}, u32[]{:S(2)}) async-start(bf16[128,64,128]{2,0,1:T(8,128)(2,1)} %copy.79), calls=%async_computation.1 | async-start | bytes 4194304 | tf_op jit(solution)/shard_map/all_to_all | solution.py:76
  125.6 1.4 copy-start.2
  152.6 14.2 %all-to-all-start.2 = ((f32[128,32,2]{0,2,1:T(2,128)}), f32[128,32,2]{0,2,1:T(2,128)S(1)}, u32[]{:S(2)}, u32[]{:S(2)}) async-start(f32[128,32,2]{0,2,1:T(2,128)} %bitcast.20), calls=%async_computation.2 | async-start | bytes 65536 | tf_op jit(solution)/shard_map/all_to_all | solution.py:80
  327.5 7.6 %copy-start = (f32[4608,128]{1,0:T(8,128)S(1)}, f32[4608,128]{1,0:T(8,128)}, u32[]{:S(2)}) copy-start(f32[4608,128]{1,0:T(8,128)} %get-tuple-element.167) | copy-start | bytes 7077892
  327.5 34.8 %all-to-all-start.6 = ((bf16[4096,2,128]{2,1,0:T(2,128)(2,1)}), bf16[4096,2,128]{2,1,0:T(2,128)(2,1)}, u32[]{:S(2)}, u32[]{:S(2)}) async-start(bf16[4096,2,128]{2,1,0:T(2,128)(2,1)} %copy.86), calls=%async_computation.6 | async-start | bytes 4194304 | tf_op jit(solution)/shard_map/all_to_all | solution.py:93
  362.2 34.0 %all-to-all-start.7 = ((f32[4096,1,128]{2,1,0:T(1,128)}), f32[4096,1,128]{2,1,0:T(1,128)S(1)}, u32[]{:S(2)}, u32[]{:S(2)}) async-start(f32[4096,1,128]{2,1,0:T(1,128)} %bitcast.138), calls=%async_computation.7 | async-start | bytes 4194304 | tf_op jit(solution)/shard_map/all_to_all | solution.py:95
  396.3 34.7 %all-to-all-start.8 = ((f32[4096,1,128]{2,1,0:T(1,128)}), f32[4096,1,128]{2,1,0:T(1,128)}, u32[]{:S(2)}, u32[]{:S(2)}) async-start(f32[4096,1,128]{2,1,0:T(1,128)} %bitcast.137), calls=%async_computation.8 | async-start | bytes 4194304 | tf_op jit(solution)/shard_map/all_to_all | solution.py:96
where the time goes:
time: 439 us; the launch traced here: 434 us
  waiting for transfers between devices  167 us (38%)
  matrix products  126 us (29%)
  starting transfers between devices  64.5 us (15%)
  local copies, waits for them, and re-layouts  57.6 us (13%)
  other arithmetic  11.5 us (3%)
  loops' own time  5.62 us (1%)
    dot_general x8, matrix products, step(): jnp.einsum('hqk,qhd->kd', prob_b, g_blk, preferred_element_type=jnp.float32)  34.6 us
    dot_general x8, matrix products, step(): jnp.einsum('qhd,kd->hqk', g_blk, v_win, preferred_element_type=jnp.float32)  29.9 us
    dot_general x8, matrix products, step(): jnp.einsum('qhd,kd->hqk', q_blk, k_win, preferred_element_type=jnp.float32)  29.5 us
    all_to_all x1, waiting for transfers between devices, per_device(): lax.all_to_all(q_grad, 'ctx', split_axis=0, concat_axis=1, tiled=True)  25.7 us
    all_to_all x1, waiting for transfers between devices, per_device(): lax.all_to_all(queries, 'ctx', split_axis=1, concat_axis=0, tiled=True)  24.5 us
    all_to_all x1, waiting for transfers between devices, per_device(): lax.all_to_all(k_grad[:, None], 'ctx', split_axis=0, concat_axis=1, tiled...  24.1 us
    all_to_all x1, waiting for transfers between devices, per_device(): lax.all_to_all(output, 'ctx', split_axis=1, concat_axis=0, tiled=True)  22.9 us
    all_to_all x1, waiting for transfers between devices, per_device(): lax.all_to_all(output_cotangent, 'ctx', split_axis=1, concat_axis=0, tile...  22.9 us
  transfers between devices with their start and end apart: 9, of which 8 were waited for; matrix products, arithmetic and copies ran while one was open for 8% of the time, Pallas kernels for 0%

commit v1 on v0

v1 whole, which is shorter than its diff:
```python
import functools

import jax
import jax.numpy as jnp
from jax import lax
from jax.experimental import pallas as pl
from jax.experimental.pallas import tpu as pltpu
from jax.sharding import PartitionSpec as P

TOK = 128
WIDTH = 128
HEADS = 64
KV = 8
HALF = KV // 2
ROWS = TOK * (HEADS // KV)
NDOC = 16
SCALE = WIDTH ** (-0.5)
LOG2E = 1.4426950408889634
F32 = jnp.float32
BF16 = jnp.bfloat16
VMEM_LIMIT = 48 * 1024 * 1024


def params(limit=VMEM_LIMIT):
    return pltpu.CompilerParams(vmem_limit_bytes=limit)


def dot(a, b, ca, cb):
    return lax.dot_general(a, b, (((ca,), (cb,)), ((), ())), preferred_element_type=F32)


def kv_prep_kernel(where, k_ref, v_ref, same_ref, flip_ref, scr):
    core = where[0] % 2
    k_t = jnp.transpose(k_ref[...].astype(F32), (1, 0, 2)).astype(BF16)
    v_t = jnp.transpose(v_ref[...].astype(F32), (1, 0, 2)).astype(BF16)
    for half in range(2):
        scr[half, :HALF] = k_t[half * HALF : (half + 1) * HALF]
        scr[half, HALF:] = v_t[half * HALF : (half + 1) * HALF]
    same_ref[...] = scr[core]
    flip_ref[...] = scr[1 - core]


def kv_prep(where, keys, values):
    half = jax.ShapeDtypeStruct((KV, TOK, WIDTH), BF16)
    return pl.pallas_call(
        kv_prep_kernel,
        out_shape=(half, half),
        in_specs=[
            pl.BlockSpec(memory_space=pltpu.SMEM),
            pl.BlockSpec(memory_space=pltpu.VMEM),
            pl.BlockSpec(memory_space=pltpu.VMEM),
        ],
        out_specs=(pl.BlockSpec(memory_space=pltpu.VMEM),) * 2,
        scratch_shapes=[pltpu.VMEM((2, KV, TOK, WIDTH), BF16)],
        compiler_params=params(),
        name="kv_prep",
    )(where, keys, values)


def delta_kernel(g_ref, o_ref, d_ref):
    prod = g_ref[...].astype(F32) * o_ref[...].astype(F32)
    ones = jnp.ones((8, WIDTH), BF16)
    for i in range(2):
        rows = prod[:, 8 * i : 8 * i + 8, :].reshape(ROWS, WIDTH)
        hi = rows.astype(BF16)
        rest = rows - hi.astype(F32)
        mid = rest.astype(BF16)
        low = (rest - mid.astype(F32)).astype(BF16)
        total = dot(ones, hi, 1, 1) + dot(ones, mid, 1, 1) + dot(ones, low, 1, 1)
        d_ref[0, i : i + 1, :] = total[:1]


def delta_rows(g, o):
    out = pl.pallas_call(
        delta_kernel,
        grid=(KV // 2,),
        out_shape=jax.ShapeDtypeStruct((KV // 2, 2, ROWS), F32),
        in_specs=[pl.BlockSpec((TOK, 16, WIDTH), lambda i: (0, i, 0))] * 2,
        out_specs=pl.BlockSpec((1, 2, ROWS), lambda i: (i, 0, 0)),
        compiler_params=params(),
        name="delta_rows",
    )(g, o)
    return out.reshape(KV, ROWS)


RANGES = {0: ((0, 128), (0, 256)), 1: ((0, 256), (0, 256)), 2: ((0, 256), (128, 256))}


def main_kernel(parts, where, lens, *refs):
    refs = list(refs)
    q_own, q_sib, g_own, g_sib, st_own, st_sib = refs[:6]
    pos = 6
    kv_in = []
    for _ in parts:
        kv_in.append((refs[pos], refs[pos + 1]))
        pos += 2
    dq_own, dq_sib = refs[pos : pos + 2]
    pos += 2
    dkv_out = []
    for _ in parts:
        dkv_out.append((refs[pos], refs[pos + 1]))
        pos += 2
    q_s, g_s, st_s, kv_s, acc_s, dq_s, lo_s = refs[pos:]
    step = pl.program_id(0)
    index = where[0]
    core = index % 2
    chip = index // 2

    @pl.when(step == 0)
    def _():
        for s in range(2):
            at = (chip * 2 + s) * TOK + lax.shift_right_logical(
                lax.broadcasted_iota(jnp.int32, (1, ROWS), 1), 3
            )
            low = jnp.zeros((1, ROWS), jnp.int32)
            end = jnp.int32(0)
            for n in range(NDOC):
                end = end + lens[n]
                low = jnp.where(at >= end, end, low)
            lo_s[s] = low

    for src, dst in ((q_own, q_s), (g_own, g_s)):
        x = src[...].astype(F32)
        for i in range(2):
            dst[core, i] = x[:, 8 * i : 8 * i + 8, :].reshape(ROWS, WIDTH).astype(BF16)
    for src, dst in ((q_sib, q_s), (g_sib, g_s)):
        x = src[...].astype(F32)
        for i in range(2):
            dst[1 - core, i] = x[:, 8 * i : 8 * i + 8, :].reshape(ROWS, WIDTH).astype(BF16)
    st_s[core] = st_own[...]
    st_s[1 - core] = st_sib[...]
    for n, (same, flip) in enumerate(kv_in):
        kv_s[n, :, :, pl.ds(pl.multiple_of(core * TOK, TOK), TOK), :] = same[...]
        kv_s[n, :, :, pl.ds(pl.multiple_of((1 - core) * TOK, TOK), TOK), :] = flip[...]
    acc_s[...] = jnp.zeros_like(acc_s)

    for i in range(2):
        for s in range(2):
            q = q_s[s, i]
            g = g_s[s, i]
            lse = st_s[s, 0, 0, i : i + 1] * LOG2E
            delta = st_s[s, 1, 0, i : i + 1]
            low = lo_s[s]
            dq = None
            for n, part in enumerate(parts):
                first, last = RANGES[part][s]
                size = last - first
                k = kv_s[n, 0, i, first:last, :]
                v = kv_s[n, 1, i, first:last, :]
                base = (chip - part) * 2 * TOK + first
                j = base + lax.broadcasted_iota(jnp.int32, (size, ROWS), 0)
                visible = j >= low
                if part == 0:
                    at = (chip * 2 + s) * TOK + lax.shift_right_logical(
                        lax.broadcasted_iota(jnp.int32, (1, ROWS), 1), 3
                    )
                    visible = visible & (j <= at)
                score = dot(k, q, 1, 1)
                prob = jnp.where(visible, jnp.exp2(score * (SCALE * LOG2E) - lse), 0.0)
                acc_s[n, 1, i, first:last, :] += dot(prob.astype(BF16), g, 1, 0)
                dprob = dot(v, g, 1, 1)
                ds = (prob * (dprob - delta)).astype(BF16)
                acc_s[n, 0, i, first:last, :] += dot(ds, q, 1, 0) * SCALE
                d = dot(k, ds, 0, 0)
                dq = d if dq is None else dq + d
            dq_s[s, :, i] = (jnp.transpose(dq) * SCALE).reshape(TOK, 8, WIDTH)

    for n, (same, flip) in enumerate(dkv_out):
        same[...] = acc_s[n, :, :, pl.ds(pl.multiple_of(core * TOK, TOK), TOK), :].astype(same.dtype)
        flip[...] = acc_s[n, :, :, pl.ds(pl.multiple_of((1 - core) * TOK, TOK), TOK), :].astype(
            flip.dtype
        )
    dq_own[...] = dq_s[core].reshape(TOK, 16, WIDTH).astype(BF16)
    dq_sib[...] = dq_s[1 - core].reshape(TOK, 16, WIDTH).astype(BF16)


def main_call(parts, where, lens, q_own, q_sib, g_own, g_sib, st_own, st_sib, kvs):
    heads = pl.BlockSpec((TOK, 16, WIDTH), lambda i, w, l: (0, 2 * (w[0] % 2) + i, 0))
    stats = pl.BlockSpec((2, 1, 2, ROWS), lambda i, w, l: (0, 2 * (w[0] % 2) + i, 0, 0))
    kv_spec = pl.BlockSpec((2, 2, TOK, WIDTH), lambda i, w, l: (0, i, 0, 0))
    dq_spec = pl.BlockSpec((TOK, 16, WIDTH), lambda i, w, l: (0, i, 0))
    dq_shape = jax.ShapeDtypeStruct((TOK, HEADS // 2, WIDTH), BF16)
    out_shape = [dq_shape, dq_shape]
    for part in parts:
        out_shape.append(
            jax.ShapeDtypeStruct((2, HALF, TOK, WIDTH), F32 if part == 0 else BF16)
        )
        out_shape.append(jax.ShapeDtypeStruct((2, HALF, TOK, WIDTH), BF16))
    flat = []
    for same, flip in kvs:
        flat += [same.reshape(2, HALF, TOK, WIDTH), flip.reshape(2, HALF, TOK, WIDTH)]
    size = len(parts)
    outs = pl.pallas_call(
        functools.partial(main_kernel, parts),
        grid_spec=pltpu.PrefetchScalarGridSpec(
            num_scalar_prefetch=2,
            grid=(2,),
            in_specs=[heads] * 4 + [stats] * 2 + [kv_spec] * len(flat),
            out_specs=[dq_spec] * 2 + [kv_spec] * len(flat),
            scratch_shapes=[
                pltpu.VMEM((2, 2, ROWS, WIDTH), BF16),
                pltpu.VMEM((2, 2, ROWS, WIDTH), BF16),
                pltpu.VMEM((2, 2, 1, 2, ROWS), F32),
                pltpu.VMEM((size, 2, 2, 2 * TOK, WIDTH), BF16),
                pltpu.VMEM((size, 2, 2, 2 * TOK, WIDTH), F32),
                pltpu.VMEM((2, TOK, 2, 8, WIDTH), F32),
                pltpu.VMEM((2, 1, ROWS), jnp.int32),
            ],
        ),
        out_shape=out_shape,
        compiler_params=params(),
        name="attention_grads",
    )(where, lens, q_own, q_sib, g_own, g_sib, st_own, st_sib, *flat)
    return outs


def final_kernel(where, own, sib, s1, f1, s2, f2, dk_ref, dv_ref, scr):
    core = where[0] % 2
    scr[core] = own[...] + s1[...].astype(F32) + s2[...].astype(F32)
    scr[1 - core] = sib[...].astype(F32) + f1[...].astype(F32) + f2[...].astype(F32)
    for which, out in enumerate((dk_ref, dv_ref)):
        x = jnp.concatenate([scr[0, which], scr[1, which]], axis=0)
        out[...] = jnp.transpose(x, (1, 0, 2)).astype(BF16)


def final_sum(where, *arrays):
    out = jax.ShapeDtypeStruct((TOK, KV, WIDTH), BF16)
    return pl.pallas_call(
        final_kernel,
        out_shape=(out, out),
        in_specs=[pl.BlockSpec(memory_space=pltpu.SMEM)]
        + [pl.BlockSpec(memory_space=pltpu.VMEM)] * 6,
        out_specs=(pl.BlockSpec(memory_space=pltpu.VMEM),) * 2,
        scratch_shapes=[pltpu.VMEM((2, 2, HALF, TOK, WIDTH), F32)],
        compiler_params=params(),
        name="final_sum",
    )(where, *arrays)


def dq_kernel(where, own, sib, out):
    core = where[0] % 2
    mine = (pl.program_id(0) // 2) == core

    @pl.when(mine)
    def _():
        out[...] = own[...]

    @pl.when(jnp.logical_not(mine))
    def _():
        out[...] = sib[...]


def dq_join(where, own, sib):
    def own_map(i, w):
        return (0, i % 2, 0)

    return pl.pallas_call(
        dq_kernel,
        grid_spec=pltpu.PrefetchScalarGridSpec(
            num_scalar_prefetch=1,
            grid=(4,),
            in_specs=[pl.BlockSpec((TOK, 16, WIDTH), own_map)] * 2,
            out_specs=pl.BlockSpec((TOK, 16, WIDTH), lambda i, w: (0, i, 0)),
        ),
        out_shape=jax.ShapeDtypeStruct((TOK, HEADS, WIDTH), BF16),
        compiler_params=params(),
        name="dq_join",
    )(where, own, sib)


def move(x, count, chips, flip):
    pairs = []
    for i in range(count):
        chip, core = divmod(i, 2)
        pairs.append((i, ((chip + chips) % (count // 2)) * 2 + (core ^ flip)))
    return lax.ppermute(x, "ctx", pairs)


def per_device(queries, keys, values, output, output_cotangent, logsumexp_rows, doc_lengths):
    count = lax.axis_size("ctx")
    index = lax.axis_index("ctx").astype(jnp.int32)
    where = index[None]
    shift = functools.partial(move, count=count)

    same, flip = kv_prep(where, keys, values)
    same1 = shift(same, chips=1, flip=0)
    flip1 = shift(flip, chips=1, flip=1)
    same2 = shift(same, chips=2, flip=0)
    flip2 = shift(flip, chips=2, flip=1)
    flip0 = shift(flip, chips=0, flip=1)
    q_sib = shift(queries, chips=0, flip=1)
    g_sib = shift(output_cotangent, chips=0, flip=1)
    delta = delta_rows(output_cotangent, output)
    lse = logsumexp_rows.reshape(TOK, KV, HEADS // KV).transpose(1, 0, 2).reshape(KV, ROWS)
    st_own = jnp.stack([lse, delta]).reshape(2, KV // 2, 2, ROWS)
    st_sib = shift(st_own, chips=0, flip=1)

    outs = main_call(
        (0, 1, 2),
        where,
        doc_lengths,
        queries,
        q_sib,
        output_cotangent,
        g_sib,
        st_own,
        st_sib,
        [(same, flip0), (same1, flip1), (same2, flip2)],
    )
    dq_own, dq_sib, d0s, d0f, d1s, d1f, d2s, d2f = outs
    r1s = shift(d1s, chips=-1, flip=0)
    r1f = shift(d1f, chips=-1, flip=1)
    r2s = shift(d2s, chips=-2, flip=0)
    r2f = shift(d2f, chips=-2, flip=1)
    r0 = shift(d0f, chips=0, flip=1)
    dq_got = shift(dq_sib, chips=0, flip=1)
    query_grad = dq_join(where, dq_own, dq_got)
    key_grad, value_grad = final_sum(where, d0s, r0, r1s, r1f, r2s, r2f)
    return (query_grad, key_grad, value_grad)


def solution(mesh):
    rows = P(("dp", "ctx"), None, None)
    return jax.shard_map(
        per_device,
        mesh=mesh,
        in_specs=(rows,) * 5 + (P(("dp", "ctx"), None), P("dp")),
        out_specs=(rows,) * 3,
        check_vma=False,
    )
```

time: 439 us -> 83.5 us (0.19); the launches traced: 434 us -> 83.3 us
  waiting for transfers between devices: 167 us -> 33.4 us
  matrix products: 126 us -> 0 us
  local copies, waits for them, and re-layouts: 57.6 us -> 5.57 us
  starting transfers between devices: 64.5 us -> 15.8 us
  Pallas kernels: 0 us -> 27.7 us
  other arithmetic: 11.5 us -> 0.03 us
  loops' own time: 5.62 us -> 0 us
    all_to_all x9 -> x0, waiting for transfers between devices: 167 us -> none  [the longest x1 25.7 us: per_device(): lax.all_to_all(q_grad, 'ctx', split_axis=0, concat_axis=1, tiled=True)]
    dot_general x40 -> x0, matrix products: 126 us -> none  [the longest x8 34.6 us: step(): jnp.einsum('hqk,qhd->kd', prob_b, g_blk, preferred_element_type=jnp.float32)]
    all_to_all x9 -> x0, starting transfers between devices: 64.5 us -> none  [the longest x1 8.27 us: per_device(): lax.all_to_all(key_slots, 'ctx', split_axis=1, concat_axis=0, tiled=True)]
    ppermute x0 -> x14, waiting for transfers between devices: none -> 33.4 us  [move(): return lax.ppermute(x, 'ctx', pairs)]
    pallas_call x0 -> x5, Pallas kernels: none -> 27.7 us  [the longest x1 21.3 us: main_call(): pl.pallas_call(functools.partial(main_kernel, parts), grid_spec=pltpu.Pre...]
    ppermute x0 -> x14, starting transfers between devices: none -> 15.8 us  [move(): return lax.ppermute(x, 'ctx', pairs)]
    unnamed x18 -> x12, local copies, waits for them, and re-layouts: 19.5 us -> 5.09 us
    dynamic_update_slice x16 -> x0, local copies, waits for them, and re-layouts: 7.16 us -> none  [group_grads(): lax.scan(step, (zeros, zeros), jnp.arange(grand_total // block, dtype=jnp...]
  transfers between devices with their start and end apart: 9 -> 14, of which waited for: 8 -> 7; matrix products, arithmetic and copies ran while one was open for 8% -> 1% of each run, Pallas kernels for 0% -> 5%
where the time goes in v1:
time: 83.5 us; the launch traced here: 83.3 us
  waiting for transfers between devices  33.4 us (40%)
  Pallas kernels  27.7 us (33%)
  starting transfers between devices  15.8 us (19%)
  local copies, waits for them, and re-layouts  5.57 us (7%)
    ppermute x14, waiting for transfers between devices, move(): return lax.ppermute(x, 'ctx', pairs)  33.4 us
    pallas_call x1, Pallas kernels, main_call(): pl.pallas_call(functools.partial(main_kernel, parts), grid_spec=pltpu.Pre...  21.3 us
    ppermute x14, starting transfers between devices, move(): return lax.ppermute(x, 'ctx', pairs)  15.8 us
    unnamed x12, local copies, waits for them, and re-layouts  5.09 us
    pallas_call x1, Pallas kernels, delta_rows(): pl.pallas_call(delta_kernel, grid=(KV // 2,), out_shape=jax.ShapeDtypeStr...  2.89 us
    pallas_call x1, Pallas kernels, dq_join(): pl.pallas_call(dq_kernel, grid_spec=pltpu.PrefetchScalarGridSpec(num_scal...  2.1 us
  transfers between devices with their start and end apart: 14, of which 7 were waited for; matrix products, arithmetic and copies ran while one was open for 1% of the time, Pallas kernels for 5%

profile of v1, /device:TPU:55, one launch (start us, length us, event | category | flops | bytes accessed | tf_op | source)
XLA Modules:
  0.0 83.3 jit_solution(15199274766133794863)
XLA Ops:
  0.6 0.8 collective-permute-start
  1.4 0.1 collective-permute-start.1
  1.5 0.0 copy-start.2
  1.5 0.9 %copy-done.2 = bf16[128,8,128]{2,1,0:T(8,128)(2,1)S(1)} copy-done((bf16[128,8,128]{2,1,0:T(8,128)(2,1)S(1)}, bf16[128,8,128]{2,1,0:T(8,128)(2,1)}, u32[]{:S(2)}) %copy-start.2) | copy-done | bytes 262168
  2.4 0.0 copy-start.3
  2.4 0.9 %copy-done.3 = bf16[128,8,128]{2,1,0:T(8,128)(2,1)S(1)} copy-done((bf16[128,8,128]{2,1,0:T(8,128)(2,1)S(1)}, bf16[128,8,128]{2,1,0:T(8,128)(2,1)}, u32[]{:S(2)}) %copy-start.3) | copy-done | bytes 262168
  3.4 0.3 kv_prep.1
  3.7 0.0 copy-start.4
  3.7 2.5 %collective-permute-start.6 = (bf16[8,128,128]{2,1,0:T(8,128)(2,1)S(1)}, bf16[8,128,128]{2,1,0:T(8,128)(2,1)S(1)}, u32[]{:S(2)}, u32[]{:S(2)}) collective-permute-start(bf16[8,128,128]{2,1,0:T(8,128)(2,1)S(1)} %get-tuple-element.15), channel_id=1, source_target_pairs={{0,4},{1,5},{2,6},{3,7},{4,8},{5,9},{6,10},{7,11},{8,12},{9,13},{1... | collective-permute-start | bytes 786440 | tf_op jit(solution)/shard_map/ppermute | solution.py:276
  6.3 1.8 %collective-permute-start.4 = (bf16[8,128,128]{2,1,0:T(8,128)(2,1)S(1)}, bf16[8,128,128]{2,1,0:T(8,128)(2,1)S(1)}, u32[]{:S(2)}, u32[]{:S(2)}) collective-permute-start(bf16[8,128,128]{2,1,0:T(8,128)(2,1)S(1)} %get-tuple-element.15), channel_id=1, source_target_pairs={{0,2},{1,3},{2,4},{3,5},{4,6},{5,7},{6,8},{7,9},{8,10},{9,11},{10,... | collective-permute-start | bytes 786440 | tf_op jit(solution)/shard_map/ppermute | solution.py:276
  8.1 0.0 copy-start
  8.1 1.6 %copy-done = bf16[128,64,128]{2,1,0:T(8,128)(2,1)S(1)} copy-done((bf16[128,64,128]{2,1,0:T(8,128)(2,1)S(1)}, bf16[128,64,128]{2,1,0:T(8,128)(2,1)}, u32[]{:S(2)}) %copy-start) | copy-done | bytes 2097176
  9.7 0.0 copy-start.1
  9.7 1.6 %copy-done.1 = bf16[128,64,128]{2,1,0:T(8,128)(2,1)S(1)} copy-done((bf16[128,64,128]{2,1,0:T(8,128)(2,1)S(1)}, bf16[128,64,128]{2,1,0:T(8,128)(2,1)}, u32[]{:S(2)}) %copy-start.1) | copy-done | bytes 2097176
  11.3 0.0 copy-start.5
  11.3 2.9 %delta_rows.1 = f32[4,2,1024]{2,1,0:T(2,128)S(1)} custom-call(bf16[128,64,128]{2,1,0:T(8,128)(2,1)S(1)} %copy-done, bf16[128,64,128]{2,1,0:T(8,128)(2,1)S(1)} %copy-done.1), custom_call_target="tpu_custom_call" | custom-call | tf_op jit(solution)/shard_map/delta_rows/pallas_call | solution.py:74
  14.2 0.0 copy-done.5
  14.2 0.2 copy.11
  14.4 0.3 stack.7
  14.7 1.1 %collective-permute-start.2 = (f32[2,4,2,1024]{3,2,1,0:T(2,128)S(1)}, f32[2,4,2,1024]{3,2,1,0:T(2,128)S(1)}, u32[]{:S(2)}, u32[]{:S(2)}) collective-permute-start(f32[2,4,2,1024]{3,2,1,0:T(2,128)S(1)} %pad_maximum_fusion.refs_4_), channel_id=1, source_target_pairs={{0,1},{1,0},{2,3},{3,2},{4,5},{5,4},{6,7},{7,6},{8,9},{9,8},{10,11... | collective-permute-start | bytes 196616 | tf_op jit(solution)/shard_map/ppermute | solution.py:276
  15.8 0.9 %collective-permute-done.2.refs_5_ = f32[2,4,2,1024]{3,2,1,0:T(2,128)S(1)} collective-permute-done((f32[2,4,2,1024]{3,2,1,0:T(2,128)S(1)}, f32[2,4,2,1024]{3,2,1,0:T(2,128)S(1)}, u32[]{:S(2)}, u32[]{:S(2)}) %collective-permute-start.2) | collective-permute-done | bytes 65568 | tf_op jit(solution)/shard_map/ppermute | solution.py:276
  16.7 0.9 %collective-permute-start.7 = (bf16[8,128,128]{2,1,0:T(8,128)(2,1)S(1)}, bf16[8,128,128]{2,1,0:T(8,128)(2,1)S(1)}, u32[]{:S(2)}, u32[]{:S(2)}) collective-permute-start(bf16[8,128,128]{2,1,0:T(8,128)(2,1)S(1)} %get-tuple-element.16), channel_id=1, source_target_pairs={{0,5},{1,4},{2,7},{3,6},{4,9},{5,8},{6,11},{7,10},{8,13},{9,12},{1... | collective-permute-start | bytes 786440 | tf_op jit(solution)/shard_map/ppermute | solution.py:276
  17.6 0.0 collective-permute-done.6
  17.6 2.5 %collective-permute-start.5 = (bf16[8,128,128]{2,1,0:T(8,128)(2,1)S(1)}, bf16[8,128,128]{2,1,0:T(8,128)(2,1)S(1)}, u32[]{:S(2)}, u32[]{:S(2)}) collective-permute-start(bf16[8,128,128]{2,1,0:T(8,128)(2,1)S(1)} %get-tuple-element.16), channel_id=1, source_target_pairs={{0,3},{1,2},{2,5},{3,4},{4,7},{5,6},{6,9},{7,8},{8,11},{9,10},{10,... | collective-permute-start | bytes 786440 | tf_op jit(solution)/shard_map/ppermute | solution.py:276
  20.1 0.0 collective-permute-done.4
  20.1 0.4 collective-permute-start.3
  20.4 6.0 %collective-permute-done.7 = bf16[8,128,128]{2,1,0:T(8,128)(2,1)S(1)} collective-permute-done((bf16[8,128,128]{2,1,0:T(8,128)(2,1)S(1)}, bf16[8,128,128]{2,1,0:T(8,128)(2,1)S(1)}, u32[]{:S(2)}, u32[]{:S(2)}) %collective-permute-start.7) | collective-permute-done | bytes 262176 | tf_op jit(solution)/shard_map/ppermute | solution.py:276
  26.4 3.6 %collective-permute-done.5 = bf16[8,128,128]{2,1,0:T(8,128)(2,1)S(1)} collective-permute-done((bf16[8,128,128]{2,1,0:T(8,128)(2,1)S(1)}, bf16[8,128,128]{2,1,0:T(8,128)(2,1)S(1)}, u32[]{:S(2)}, u32[]{:S(2)}) %collective-permute-start.5) | collective-permute-done | bytes 262176 | tf_op jit(solution)/shard_map/ppermute | solution.py:276
  30.0 0.0 collective-permute-done.3
  30.0 0.0 collective-permute-done.refs_1_
  30.0 0.0 collective-permute-done.1.refs_3_
  30.0 0.0 copy-done.4
  30.1 21.3 %attention_grads.1 = (bf16[128,32,128]{2,1,0:T(8,128)(2,1)S(1)}, bf16[128,32,128]{2,1,0:T(8,128)(2,1)S(1)}, f32[2,4,128,128]{3,2,1,0:T(8,128)S(1)}, bf16[2,4,128...) custom-call(s32[1]{0:T(128)} %bitcast.where, ...), custom_call_target="tpu_custom_call" | custom-call | tf_op jit(solution)/shard_map/attention_grads/pallas_call | solution.py:193
  51.3 0.3 collective-permute-start.8
  51.7 0.2 collective-permute-start.9
  51.9 1.9 %collective-permute-start.10 = (bf16[2,4,128,128]{3,2,1,0:T(8,128)(2,1)S(1)}, bf16[2,4,128,128]{3,2,1,0:T(8,128)(2,1)S(1)}, u32[]{:S(2)}, u32[]{:S(2)}) collective-permute-start(bf16[2,4,128,128]{3,2,1,0:T(8,128)(2,1)S(1)} %get-tuple-element.21), channel_id=1, source_target_pairs={{0,30},{1,31},{2,0},{3,1},{4,2},{5,3},{6,4},{7,5},{8,6},{9,7},{10,... | collective-permute-start | bytes 786440 | tf_op jit(solution)/shard_map/ppermute | solution.py:276
  53.8 0.5 collective-permute-start.11
  54.4 1.4 %collective-permute-start.12 = (bf16[2,4,128,128]{3,2,1,0:T(8,128)(2,1)S(1)}, bf16[2,4,128,128]{3,2,1,0:T(8,128)(2,1)S(1)}, u32[]{:S(2)}, u32[]{:S(2)}) collective-permute-start(bf16[2,4,128,128]{3,2,1,0:T(8,128)(2,1)S(1)} %get-tuple-element.23), channel_id=1, source_target_pairs={{0,28},{1,29},{2,30},{3,31},{4,0},{5,1},{6,2},{7,3},{8,4},{9,5},{1... | collective-permute-start | bytes 786440 | tf_op jit(solution)/shard_map/ppermute | solution.py:276
  55.8 0.0 collective-permute-done.9.sib
  55.8 1.4 %collective-permute-start.13 = (bf16[2,4,128,128]{3,2,1,0:T(8,128)(2,1)S(1)}, bf16[2,4,128,128]{3,2,1,0:T(8,128)(2,1)S(1)}, u32[]{:S(2)}, u32[]{:S(2)}) collective-permute-start(bf16[2,4,128,128]{3,2,1,0:T(8,128)(2,1)S(1)} %get-tuple-element.24), channel_id=1, source_target_pairs={{0,29},{1,28},{2,31},{3,30},{4,1},{5,0},{6,3},{7,2},{8,5},{9,4},{1... | collective-permute-start | bytes 786440 | tf_op jit(solution)/shard_map/ppermute | solution.py:276
  57.1 4.5 %collective-permute-done.10.s1 = bf16[2,4,128,128]{3,2,1,0:T(8,128)(2,1)S(1)} collective-permute-done((bf16[2,4,128,128]{3,2,1,0:T(8,128)(2,1)S(1)}, bf16[2,4,128,128]{3,2,1,0:T(8,128)(2,1)S(1)}, u32[]{:S(2)}, u32[]{:S(2)}) %collective-permute-start.10) | collective-permute-done | bytes 262176 | tf_op jit(solution)/shard_map/ppermute | solution.py:276
  61.7 6.0 %collective-permute-done.11.f1 = bf16[2,4,128,128]{3,2,1,0:T(8,128)(2,1)S(1)} collective-permute-done((bf16[2,4,128,128]{3,2,1,0:T(8,128)(2,1)S(1)}, bf16[2,4,128,128]{3,2,1,0:T(8,128)(2,1)S(1)}, u32[]{:S(2)}, u32[]{:S(2)}) %collective-permute-start.11) | collective-permute-done | bytes 262176 | tf_op jit(solution)/shard_map/ppermute | solution.py:276
  67.7 6.3 %collective-permute-done.12.s2 = bf16[2,4,128,128]{3,2,1,0:T(8,128)(2,1)S(1)} collective-permute-done((bf16[2,4,128,128]{3,2,1,0:T(8,128)(2,1)S(1)}, bf16[2,4,128,128]{3,2,1,0:T(8,128)(2,1)S(1)}, u32[]{:S(2)}, u32[]{:S(2)}) %collective-permute-start.12) | collective-permute-done | bytes 262176 | tf_op jit(solution)/shard_map/ppermute | solution.py:276
  73.9 6.1 %collective-permute-done.13.f2 = bf16[2,4,128,128]{3,2,1,0:T(8,128)(2,1)S(1)} collective-permute-done((bf16[2,4,128,128]{3,2,1,0:T(8,128)(2,1)S(1)}, bf16[2,4,128,128]{3,2,1,0:T(8,128)(2,1)S(1)}, u32[]{:S(2)}, u32[]{:S(2)}) %collective-permute-start.13) | collective-permute-done | bytes 262176 | tf_op jit(solution)/shard_map/ppermute | solution.py:276
  80.0 1.2 %final_sum.1 = (bf16[128,8,128]{2,1,0:T(8,128)(2,1)}, bf16[128,8,128]{2,1,0:T(8,128)(2,1)}) custom-call(s32[1]{0:T(128)} %bitcast.where, f32[2,4,128,128]{3,2,1,0:T(8,128)S(1)} %get-tuple-element.19.own, bf16[2,4,128,128]{3,2,1,0:T(8,128)(2,1)S(1)} %collective-permute-done.9.sib, bf16[2,4,128,128]{3,2,1,0:T(8,128)(2,1)S(1)} %collective-permute-done.10.s1, ...), custom_call_target="tpu_custom_call" | custom-call | tf_op jit(solution)/shard_map/final_sum/pallas_call | solution.py:228
  81.2 0.0 collective-permute-done.8.sib
  81.2 2.1 %dq_join.1 = bf16[128,64,128]{2,1,0:T(8,128)(2,1)} custom-call(s32[1]{0:T(128)} %bitcast.where, bf16[128,32,128]{2,1,0:T(8,128)(2,1)S(1)} %get-tuple-element.17.own, bf16[128,32,128]{2,1,0:T(8,128)(2,1)S(1)} %collective-permute-done.8.sib), custom_call_target="tpu_custom_call" | custom-call | tf_op jit(solution)/shard_map/dq_join/pallas_call | solution.py:257
  (1 shorter events, 0.0 us)
Async XLA Ops:
  0.6 29.4 %collective-permute-start = (bf16[128,64,128]{2,1,0:T(8,128)(2,1)}, bf16[128,64,128]{2,1,0:T(8,128)(2,1)}, u32[]{:S(2)}, u32[]{:S(2)}) collective-permute-start(bf16[128,64,128]{2,1,0:T(8,128)(2,1)} %refs_0_.1), channel_id=1, source_target_pairs={{0,1},{1,0},{2,3},{3,2},{4,5},{5,4},{6,7},{7,6},{8,9},{9,8},{10,11... | collective-permute-start | bytes 6291464 | tf_op jit(solution)/shard_map/ppermute | solution.py:276
  1.4 28.7 %collective-permute-start.1 = (bf16[128,64,128]{2,1,0:T(8,128)(2,1)}, bf16[128,64,128]{2,1,0:T(8,128)(2,1)}, u32[]{:S(2)}, u32[]{:S(2)}) collective-permute-start(bf16[128,64,128]{2,1,0:T(8,128)(2,1)} %refs_2_.1), channel_id=1, source_target_pairs={{0,1},{1,0},{2,3},{3,2},{4,5},{5,4},{6,7},{7,6},{8,9},{9,8},{10,11... | collective-permute-start | bytes 6291464 | tf_op jit(solution)/shard_map/ppermute | solution.py:276
  1.5 0.9 %copy-start.2 = (bf16[128,8,128]{2,1,0:T(8,128)(2,1)S(1)}, bf16[128,8,128]{2,1,0:T(8,128)(2,1)}, u32[]{:S(2)}) copy-start(bf16[128,8,128]{2,1,0:T(8,128)(2,1)} %k_ref.1) | copy-start | bytes 786436
  2.4 0.9 %copy-start.3 = (bf16[128,8,128]{2,1,0:T(8,128)(2,1)S(1)}, bf16[128,8,128]{2,1,0:T(8,128)(2,1)}, u32[]{:S(2)}) copy-start(bf16[128,8,128]{2,1,0:T(8,128)(2,1)} %v_ref.1) | copy-start | bytes 786436
  3.7 26.3 %copy-start.4 = (s32[16]{0:T(128)S(1)}, s32[16]{0:T(128)}, u32[]{:S(2)}) copy-start(s32[16]{0:T(128)} %lens.1) | copy-start | bytes 196
  3.7 13.9 %collective-permute-start.6 = (bf16[8,128,128]{2,1,0:T(8,128)(2,1)S(1)}, bf16[8,128,128]{2,1,0:T(8,128)(2,1)S(1)}, u32[]{:S(2)}, u32[]{:S(2)}) collective-permute-start(bf16[8,128,128]{2,1,0:T(8,128)(2,1)S(1)} %get-tuple-element.15), channel_id=1, source_target_pairs={{0,4},{1,5},{2,6},{3,7},{4,8},{5,9},{6,10},{7,11},{8,12},{9,13},{1... | collective-permute-start | bytes 786440 | tf_op jit(solution)/shard_map/ppermute | solution.py:276
  6.3 13.8 %collective-permute-start.4 = (bf16[8,128,128]{2,1,0:T(8,128)(2,1)S(1)}, bf16[8,128,128]{2,1,0:T(8,128)(2,1)S(1)}, u32[]{:S(2)}, u32[]{:S(2)}) collective-permute-start(bf16[8,128,128]{2,1,0:T(8,128)(2,1)S(1)} %get-tuple-element.15), channel_id=1, source_target_pairs={{0,2},{1,3},{2,4},{3,5},{4,6},{5,7},{6,8},{7,9},{8,10},{9,11},{10,... | collective-permute-start | bytes 786440 | tf_op jit(solution)/shard_map/ppermute | solution.py:276
  8.1 1.6 %copy-start = (bf16[128,64,128]{2,1,0:T(8,128)(2,1)S(1)}, bf16[128,64,128]{2,1,0:T(8,128)(2,1)}, u32[]{:S(2)}) copy-start(bf16[128,64,128]{2,1,0:T(8,128)(2,1)} %refs_2_.1) | copy-start | bytes 6291460
  9.7 1.6 %copy-start.1 = (bf16[128,64,128]{2,1,0:T(8,128)(2,1)S(1)}, bf16[128,64,128]{2,1,0:T(8,128)(2,1)}, u32[]{:S(2)}) copy-start(bf16[128,64,128]{2,1,0:T(8,128)(2,1)} %o_ref.1) | copy-start | bytes 6291460
  11.3 2.9 %copy-start.5 = (f32[128,64]{0,1:T(8,128)S(1)}, f32[128,64]{0,1:T(8,128)}, u32[]{:S(2)}) copy-start(f32[128,64]{0,1:T(8,128)} %param.12) | copy-start | bytes 98308
  14.7 2.0 %collective-permute-start.2 = (f32[2,4,2,1024]{3,2,1,0:T(2,128)S(1)}, f32[2,4,2,1024]{3,2,1,0:T(2,128)S(1)}, u32[]{:S(2)}, u32[]{:S(2)}) collective-permute-start(f32[2,4,2,1024]{3,2,1,0:T(2,128)S(1)} %pad_maximum_fusion.refs_4_), channel_id=1, source_target_pairs={{0,1},{1,0},{2,3},{3,2},{4,5},{5,4},{6,7},{7,6},{8,9},{9,8},{10,11... | collective-permute-start | bytes 196616 | tf_op jit(solution)/shard_map/ppermute | solution.py:276
  16.7 9.8 %collective-permute-start.7 = (bf16[8,128,128]{2,1,0:T(8,128)(2,1)S(1)}, bf16[8,128,128]{2,1,0:T(8,128)(2,1)S(1)}, u32[]{:S(2)}, u32[]{:S(2)}) collective-permute-start(bf16[8,128,128]{2,1,0:T(8,128)(2,1)S(1)} %get-tuple-element.16), channel_id=1, source_target_pairs={{0,5},{1,4},{2,7},{3,6},{4,9},{5,8},{6,11},{7,10},{8,13},{9,12},{1... | collective-permute-start | bytes 786440 | tf_op jit(solution)/shard_map/ppermute | solution.py:276
  17.6 12.4 %collective-permute-start.5 = (bf16[8,128,128]{2,1,0:T(8,128)(2,1)S(1)}, bf16[8,128,128]{2,1,0:T(8,128)(2,1)S(1)}, u32[]{:S(2)}, u32[]{:S(2)}) collective-permute-start(bf16[8,128,128]{2,1,0:T(8,128)(2,1)S(1)} %get-tuple-element.16), channel_id=1, source_target_pairs={{0,3},{1,2},{2,5},{3,4},{4,7},{5,6},{6,9},{7,8},{8,11},{9,10},{10,... | collective-permute-start | bytes 786440 | tf_op jit(solution)/shard_map/ppermute | solution.py:276
  20.1 10.0 %collective-permute-start.3 = (bf16[8,128,128]{2,1,0:T(8,128)(2,1)S(1)}, bf16[8,128,128]{2,1,0:T(8,128)(2,1)S(1)}, u32[]{:S(2)}, u32[]{:S(2)}) collective-permute-start(bf16[8,128,128]{2,1,0:T(8,128)(2,1)S(1)} %get-tuple-element.16), channel_id=1, source_target_pairs={{0,1},{1,0},{2,3},{3,2},{4,5},{5,4},{6,7},{7,6},{8,9},{9,8},{10,11... | collective-permute-start | bytes 786440 | tf_op jit(solution)/shard_map/ppermute | solution.py:276
  51.3 29.9 %collective-permute-start.8 = (bf16[128,32,128]{2,1,0:T(8,128)(2,1)S(1)}, bf16[128,32,128]{2,1,0:T(8,128)(2,1)S(1)}, u32[]{:S(2)}, u32[]{:S(2)}) collective-permute-start(bf16[128,32,128]{2,1,0:T(8,128)(2,1)S(1)} %get-tuple-element.18), channel_id=1, source_target_pairs={{0,1},{1,0},{2,3},{3,2},{4,5},{5,4},{6,7},{7,6},{8,9},{9,8},{10,11... | collective-permute-start | bytes 3145736 | tf_op jit(solution)/shard_map/ppermute | solution.py:276
  51.7 4.1 %collective-permute-start.9 = (bf16[2,4,128,128]{3,2,1,0:T(8,128)(2,1)S(1)}, bf16[2,4,128,128]{3,2,1,0:T(8,128)(2,1)S(1)}, u32[]{:S(2)}, u32[]{:S(2)}) collective-permute-start(bf16[2,4,128,128]{3,2,1,0:T(8,128)(2,1)S(1)} %get-tuple-element.20), channel_id=1, source_target_pairs={{0,1},{1,0},{2,3},{3,2},{4,5},{5,4},{6,7},{7,6},{8,9},{9,8},{10,11... | collective-permute-start | bytes 786440 | tf_op jit(solution)/shard_map/ppermute | solution.py:276
  51.9 9.7 %collective-permute-start.10 = (bf16[2,4,128,128]{3,2,1,0:T(8,128)(2,1)S(1)}, bf16[2,4,128,128]{3,2,1,0:T(8,128)(2,1)S(1)}, u32[]{:S(2)}, u32[]{:S(2)}) collective-permute-start(bf16[2,4,128,128]{3,2,1,0:T(8,128)(2,1)S(1)} %get-tuple-element.21), channel_id=1, source_target_pairs={{0,30},{1,31},{2,0},{3,1},{4,2},{5,3},{6,4},{7,5},{8,6},{9,7},{10,... | collective-permute-start | bytes 786440 | tf_op jit(solution)/shard_map/ppermute | solution.py:276
  53.8 13.8 %collective-permute-start.11 = (bf16[2,4,128,128]{3,2,1,0:T(8,128)(2,1)S(1)}, bf16[2,4,128,128]{3,2,1,0:T(8,128)(2,1)S(1)}, u32[]{:S(2)}, u32[]{:S(2)}) collective-permute-start(bf16[2,4,128,128]{3,2,1,0:T(8,128)(2,1)S(1)} %get-tuple-element.22), channel_id=1, source_target_pairs={{0,31},{1,30},{2,1},{3,0},{4,3},{5,2},{6,5},{7,4},{8,7},{9,6},{10,... | collective-permute-start | bytes 786440 | tf_op jit(solution)/shard_map/ppermute | solution.py:276
  54.4 19.6 %collective-permute-start.12 = (bf16[2,4,128,128]{3,2,1,0:T(8,128)(2,1)S(1)}, bf16[2,4,128,128]{3,2,1,0:T(8,128)(2,1)S(1)}, u32[]{:S(2)}, u32[]{:S(2)}) collective-permute-start(bf16[2,4,128,128]{3,2,1,0:T(8,128)(2,1)S(1)} %get-tuple-element.23), channel_id=1, source_target_pairs={{0,28},{1,29},{2,30},{3,31},{4,0},{5,1},{6,2},{7,3},{8,4},{9,5},{1... | collective-permute-start | bytes 786440 | tf_op jit(solution)/shard_map/ppermute | solution.py:276
  55.8 24.2 %collective-permute-start.13 = (bf16[2,4,128,128]{3,2,1,0:T(8,128)(2,1)S(1)}, bf16[2,4,128,128]{3,2,1,0:T(8,128)(2,1)S(1)}, u32[]{:S(2)}, u32[]{:S(2)}) collective-permute-start(bf16[2,4,128,128]{3,2,1,0:T(8,128)(2,1)S(1)} %get-tuple-element.24), channel_id=1, source_target_pairs={{0,29},{1,28},{2,31},{3,30},{4,1},{5,0},{6,3},{7,2},{8,5},{9,4},{1... | collective-permute-start | bytes 786440 | tf_op jit(solution)/shard_map/ppermute | solution.py:276

commit v2 on v0

v2 whole, which is shorter than its diff:
```python
import functools

import jax
import jax.numpy as jnp
from jax import lax
from jax.experimental import pallas as pl
from jax.experimental.pallas import tpu as pltpu
from jax.sharding import PartitionSpec as P

TOK = 128
WIDTH = 128
HEADS = 64
KV = 8
HALF = KV // 2
ROWS = TOK * (HEADS // KV)
NDOC = 16
SCALE = WIDTH ** (-0.5)
LOG2E = 1.4426950408889634
F32 = jnp.float32
BF16 = jnp.bfloat16
VMEM_LIMIT = 48 * 1024 * 1024
PACK_VMEM = 62 * 1024 * 1024
PART_VMEM = (VMEM_LIMIT, VMEM_LIMIT, VMEM_LIMIT)


def params(limit=VMEM_LIMIT):
    return pltpu.CompilerParams(vmem_limit_bytes=limit)


def dot(a, b, ca, cb):
    return lax.dot_general(a, b, (((ca,), (cb,)), ((), ())), preferred_element_type=F32)


PACK = 2 * ROWS + 2 * TOK + 48


def split3(x):
    hi = x.astype(BF16)
    rest = x - hi.astype(F32)
    mid = rest.astype(BF16)
    low = (rest - mid.astype(F32)).astype(BF16)
    return hi, mid, low


def fold(row):
    return jnp.concatenate([row[:, c * WIDTH : (c + 1) * WIDTH] for c in range(8)], axis=0)


def unfold(block):
    return jnp.concatenate([block[c : c + 1] for c in range(8)], axis=1)


def spread_lse(lse_ref, lse_s):
    row = lax.broadcasted_iota(jnp.int32, (TOK, ROWS), 1)
    tok = lax.broadcasted_iota(jnp.int32, (TOK, ROWS), 0)
    spread = jnp.where(lax.shift_right_logical(row, 3) == tok, 1.0, 0.0).astype(BF16)
    head = lax.broadcasted_iota(jnp.int32, (8, ROWS), 0)
    pick = head == (lax.broadcasted_iota(jnp.int32, (8, ROWS), 1) & 7)
    for n, term in enumerate(split3(lse_ref[...])):
        full = dot(term, spread, 1, 0)
        for h in range(KV):
            rows = jnp.where(pick, full[8 * h : 8 * h + 8], 0.0)
            lse_s[h, n : n + 1] = jnp.sum(rows, axis=0, keepdims=True)


def row_sums(x):
    hi = x.astype(BF16)
    mid = (x - hi.astype(F32)).astype(BF16)
    ones = jnp.ones((2 * WIDTH, WIDTH), BF16)
    total = dot(jnp.concatenate([hi, mid], axis=1), ones, 1, 0)
    eye = lax.broadcasted_iota(jnp.int32, (WIDTH, WIDTH), 0) == lax.broadcasted_iota(
        jnp.int32, (WIDTH, WIDTH), 1
    )
    rows = []
    for c in range(8):
        block = jnp.where(eye, total[c * WIDTH : (c + 1) * WIDTH], 0.0)
        rows.append(jnp.sum(block, axis=0, keepdims=True))
    return jnp.concatenate(rows, axis=0)


def emit_pack(out, q_ref, g_ref, o_ref, lse_s, half, kv):
    step = pl.program_id(0)
    q = q_ref[...].astype(F32)
    g = g_ref[...].astype(F32)
    prod = g * o_ref[...].astype(F32)
    for i in range(2):
        heads = slice(8 * i, 8 * i + 8)
        out[i, :ROWS] = q[:, heads, :].reshape(ROWS, WIDTH).astype(BF16)
        out[i, ROWS : 2 * ROWS] = g[:, heads, :].reshape(ROWS, WIDTH).astype(BF16)
        out[i, 2 * ROWS : 2 * ROWS + TOK] = kv(0, i)
        out[i, 2 * ROWS + TOK : 2 * ROWS + 2 * TOK] = kv(1, i)
        delta = split3(row_sums(prod[:, heads, :].reshape(ROWS, WIDTH)))
        lse = lse_s[half * HALF + 2 * step + i]
        rows = [fold(lse[n : n + 1]) for n in range(3)] + [t.astype(F32) for t in delta]
        out[i, 2 * ROWS + 2 * TOK :] = jnp.concatenate(rows, axis=0).astype(BF16)


def sib_kernel(where, q, g, o, lse_ref, k_ref, v_ref, out, same_ref, flip_ref, lse_s, kv_s):
    step = pl.program_id(0)
    core = where[0] % 2

    @pl.when(step == 0)
    def _():
        for n, ref in enumerate((k_ref, v_ref)):
            x = jnp.transpose(ref[...].astype(F32), (1, 0, 2)).astype(BF16)
            kv_s[0, n] = x[:HALF]
            kv_s[1, n] = x[HALF:]
        same_ref[...] = kv_s[core]
        flip_ref[...] = kv_s[1 - core]
        spread_lse(lse_ref, lse_s)

    emit_pack(out, q, g, o, lse_s, 1 - core, lambda n, i: kv_s[1 - core, n, 2 * step + i])


def own_kernel(where, q, g, o, lse_ref, same_ref, out, lse_s):
    @pl.when(pl.program_id(0) == 0)
    def _():
        spread_lse(lse_ref, lse_s)

    emit_pack(out, q, g, o, lse_s, where[0] % 2, lambda n, i: same_ref[n, i])


def pack_call(kernel, flip, where, args, in_specs, out_shape, out_specs, scratch, name):
    def heads(i, w):
        core = w[0] % 2
        return (0, 2 * (1 - core if flip else core) + i, 0)

    raw = pl.BlockSpec((TOK, 16, WIDTH), heads)
    pack_shape = jax.ShapeDtypeStruct((HALF, PACK, WIDTH), BF16)
    return pl.pallas_call(
        kernel,
        grid_spec=pltpu.PrefetchScalarGridSpec(
            num_scalar_prefetch=1,
            grid=(2,),
            in_specs=[raw, raw, raw, pl.BlockSpec((HEADS, TOK), lambda i, w: (0, 0))] + in_specs,
            out_specs=[pl.BlockSpec((2, PACK, WIDTH), lambda i, w: (i, 0, 0))] + out_specs,
            scratch_shapes=[pltpu.VMEM((KV, 3, ROWS), F32)] + scratch,
        ),
        out_shape=[pack_shape] + out_shape,
        compiler_params=params(PACK_VMEM),
        name=name,
    )(where, *args)


def pack_sib(where, q, g, o, lse, k, v):
    full = pl.BlockSpec((TOK, KV, WIDTH), lambda i, w: (0, 0, 0))
    kv = pl.BlockSpec((2, HALF, TOK, WIDTH), lambda i, w: (0, 0, 0, 0))
    shape = jax.ShapeDtypeStruct((2, HALF, TOK, WIDTH), BF16)
    scratch = [pltpu.VMEM((2, 2, HALF, TOK, WIDTH), BF16)]
    args = (q, g, o, lse, k, v)
    return pack_call(
        sib_kernel, True, where, args, [full] * 2, [shape] * 2, [kv] * 2, scratch, "pack_sib"
    )


def pack_own(where, q, g, o, lse, same):
    kv = pl.BlockSpec((2, 2, TOK, WIDTH), lambda i, w: (0, i, 0, 0))
    args = (q, g, o, lse, same)
    return pack_call(own_kernel, False, where, args, [kv], [], [], [], "pack_own")[0]


RANGES = {0: ((0, 128), (0, 256)), 1: ((0, 256), (0, 256)), 2: ((0, 256), (128, 256))}
CHUNK = 1024


def positions(chip, s):
    at = lax.shift_right_logical(lax.broadcasted_iota(jnp.int32, (1, ROWS), 1), 3)
    return at + (chip * 2 + s) * TOK


def doc_starts(lens, at):
    low = jnp.zeros((1, ROWS), jnp.int32)
    end = jnp.int32(0)
    for n in range(NDOC):
        end = end + lens[n]
        low = jnp.where(at >= end, end, low)
    return low


def grads(part, chip, s, k, v, q, g, lse, delta, low, first, emit_dq):
    size = k.shape[0]
    base = (chip - part) * 2 * TOK + first
    dk = dv = None
    at = positions(chip, s) if part == 0 else None
    for r in range(0, ROWS, CHUNK):
        cols = slice(r, r + CHUNK)
        qc = q[cols]
        gc = g[cols]
        j = base + lax.broadcasted_iota(jnp.int32, (size, CHUNK), 0)
        visible = j >= low[:, cols]
        if part == 0:
            visible = visible & (j <= at[:, cols])
        score = dot(k, qc, 1, 1)
        prob = jnp.where(visible, jnp.exp2(score * (SCALE * LOG2E) - lse[:, cols]), 0.0)
        dvc = dot(prob.astype(BF16), gc, 1, 0)
        dprob = dot(v, gc, 1, 1)
        ds = (prob * (dprob - delta[:, cols])).astype(BF16)
        dkc = dot(ds, qc, 1, 0)
        dk = dkc if dk is None else dk + dkc
        dv = dvc if dv is None else dv + dvc
        emit_dq(cols, dot(k, ds, 0, 0))
    return dk * SCALE, dv


def phase_kernel(part, heads, where, lens, *refs):
    own, sib = refs[:2]
    qg_s, st_s, kv_s, acc_s, dq_s = refs[-5:]
    index = where[0]
    core = index % 2
    chip = index // 2
    own_at = pl.ds(pl.multiple_of(core * TOK, TOK), TOK)
    sib_at = pl.ds(pl.multiple_of((1 - core) * TOK, TOK), TOK)
    for half, src in ((core, own), (1 - core, sib)):
        qg_s[half] = src[:, : 2 * ROWS, :]
        for i in range(heads):
            st = src[i, 2 * ROWS + 2 * TOK :, :].astype(F32)
            st_s[half, i, 0:1] = unfold(st[0:8] + st[8:16] + st[16:24]) * LOG2E
            st_s[half, i, 1:2] = unfold(st[24:32] + st[32:40] + st[40:48])
    if part == 0:
        dq_out, d_same, d_flip = refs[2:5]
        for half, src in ((own_at, own), (sib_at, sib)):
            kv_s[0, :, half, :] = src[:, 2 * ROWS : 2 * ROWS + TOK, :]
            kv_s[1, :, half, :] = src[:, 2 * ROWS + TOK : 2 * ROWS + 2 * TOK, :]
    else:
        same, flip, dq_in = refs[2:5]
        kv_s[:, :, own_at, :] = same[...]
        kv_s[:, :, sib_at, :] = flip[...]
        if part == 1:
            dq_out, d_same, d_flip = refs[5:8]
        else:
            dq_own, *back, d_same, d_flip = refs[5:12]
    if part != 1:
        acc_s[...] = jnp.zeros_like(acc_s)

    for s in range(2):
        low = doc_starts(lens, positions(chip, s))
        for i in range(heads):
            first, last = RANGES[part][s]

            def emit(cols, d):
                if part == 0:
                    dq_out[s, i, :, cols] = d
                elif part == 1:
                    dq_out[s, i, :, cols] = dq_in[s, i, :, cols] + d
                else:
                    full = jnp.transpose(dq_in[s, i, :, cols] + d) * SCALE
                    dq_s[s, i, cols, :] = full.astype(BF16)

            dk, dv = grads(
                part,
                chip,
                s,
                kv_s[0, i, first:last, :],
                kv_s[1, i, first:last, :],
                qg_s[s, i, :ROWS],
                qg_s[s, i, ROWS:],
                st_s[s, i, 0:1],
                st_s[s, i, 1:2],
                low,
                first,
                emit,
            )
            fresh = part == 1 and s == 0
            acc_s[0, i, first:last, :] = dk if fresh else acc_s[0, i, first:last, :] + dk
            acc_s[1, i, first:last, :] = dv if fresh else acc_s[1, i, first:last, :] + dv

    d_same[...] = acc_s[:, :, own_at, :].astype(d_same.dtype)
    d_flip[...] = acc_s[:, :, sib_at, :].astype(d_flip.dtype)
    if part == 2:
        dq_own[...] = dq_s[core]
        for n in range(HALF // heads):

            @pl.when(pl.program_id(0) == n)
            def _():
                for i in range(heads):
                    back[n * heads + i][...] = dq_s[1 - core, i]


def phase(part, where, lens, own, sib, same=None, flip=None, dq=None, heads=2):
    pack_spec = pl.BlockSpec((heads, PACK, WIDTH), lambda i, w, l: (i, 0, 0))
    kv_spec = pl.BlockSpec((2, heads, TOK, WIDTH), lambda i, w, l: (0, i, 0, 0))
    dq_spec = pl.BlockSpec((2, heads, WIDTH, ROWS), lambda i, w, l: (0, i, 0, 0))
    dq_shape = jax.ShapeDtypeStruct((2, HALF, WIDTH, ROWS), F32)
    kv_shape = jax.ShapeDtypeStruct((2, HALF, TOK, WIDTH), BF16)
    args = [own, sib]
    in_specs = [pack_spec, pack_spec]
    if part == 0:
        out_shape = [dq_shape, jax.ShapeDtypeStruct((2, HALF, TOK, WIDTH), F32), kv_shape]
        out_specs = [dq_spec, kv_spec, kv_spec]
    else:
        args += [same, flip, dq]
        in_specs += [kv_spec, kv_spec, dq_spec]
        if part == 1:
            out_shape = [dq_shape, kv_shape, kv_shape]
            out_specs = [dq_spec, kv_spec, kv_spec]
        else:
            out_shape = [
                jax.ShapeDtypeStruct((HALF, ROWS, WIDTH), BF16),
                *[jax.ShapeDtypeStruct((ROWS, WIDTH), BF16)] * HALF,
                kv_shape,
                kv_shape,
            ]
            out_specs = [
                pl.BlockSpec((heads, ROWS, WIDTH), lambda i, w, l: (i, 0, 0)),
                *[pl.BlockSpec((ROWS, WIDTH), lambda i, w, l: (0, 0))] * HALF,
                kv_spec,
                kv_spec,
            ]
    return pl.pallas_call(
        functools.partial(phase_kernel, part, heads),
        grid_spec=pltpu.PrefetchScalarGridSpec(
            num_scalar_prefetch=2,
            grid=(HALF // heads,),
            in_specs=in_specs,
            out_specs=out_specs,
            scratch_shapes=[
                pltpu.VMEM((2, heads, 2 * ROWS, WIDTH), BF16),
                pltpu.VMEM((2, heads, 2, ROWS), F32),
                pltpu.VMEM((2, heads, 2 * TOK, WIDTH), BF16),
                pltpu.VMEM((2, heads, 2 * TOK, WIDTH), F32),
                pltpu.VMEM((2, heads, ROWS, WIDTH), BF16),
            ],
        ),
        out_shape=out_shape,
        compiler_params=params(PART_VMEM[part]),
        name=f"grads_part{part}",
    )(where, lens, *args)


def near_kernel(own, s1, f1, r0, out):
    out[0] = own[...] + s1[...].astype(F32)
    out[1] = f1[...].astype(F32) + r0[...].astype(F32)


def near_sum(own, s1, f1, r0):
    spec = pl.BlockSpec((1, HALF, TOK, WIDTH), lambda i: (i, 0, 0, 0))
    return pl.pallas_call(
        near_kernel,
        grid=(2,),
        out_shape=jax.ShapeDtypeStruct((2, 2, HALF, TOK, WIDTH), F32),
        in_specs=[spec] * 4,
        out_specs=pl.BlockSpec((2, 1, HALF, TOK, WIDTH), lambda i: (0, i, 0, 0, 0)),
        compiler_params=params(),
        name="near_sum",
    )(own, s1, f1, r0)


def final_kernel(where, near, s2, f2, dk_ref, dv_ref, scr):
    core = where[0] % 2
    for which, out in enumerate((dk_ref, dv_ref)):
        scr[core] = near[0, which] + s2[which].astype(F32)
        scr[1 - core] = near[1, which] + f2[which].astype(F32)
        x = jnp.concatenate([scr[0], scr[1]], axis=0)
        out[...] = jnp.transpose(x, (1, 0, 2)).astype(BF16)


def final_sum(where, near, s2, f2):
    out = jax.ShapeDtypeStruct((TOK, KV, WIDTH), BF16)
    kv = pl.BlockSpec((2, HALF, TOK, WIDTH), lambda i, w: (0, 0, 0, 0))
    full = pl.BlockSpec((TOK, KV, WIDTH), lambda i, w: (0, 0, 0))
    return pl.pallas_call(
        final_kernel,
        grid_spec=pltpu.PrefetchScalarGridSpec(
            num_scalar_prefetch=1,
            grid=(1,),
            in_specs=[
                pl.BlockSpec((2, 2, HALF, TOK, WIDTH), lambda i, w: (0, 0, 0, 0, 0)),
                kv,
                kv,
            ],
            out_specs=[full, full],
            scratch_shapes=[pltpu.VMEM((2, HALF, TOK, WIDTH), F32)],
        ),
        out_shape=(out, out),
        compiler_params=params(),
        name="final_sum",
    )(where, near, s2, f2)


def join_kernel(where, own, b0, b1, b2, b3, out):
    step = pl.program_id(0)
    mine = (step // 2) == where[0] % 2

    def emit(x0, x1):
        x = [x.astype(F32).reshape(TOK, 8, WIDTH) for x in (x0, x1)]
        out[...] = jnp.concatenate(x, axis=1).astype(BF16)

    @pl.when(mine)
    def _():
        emit(own[0], own[1])

    @pl.when(jnp.logical_not(mine) & (step % 2 == 0))
    def _():
        emit(b0[...], b1[...])

    @pl.when(jnp.logical_not(mine) & (step % 2 == 1))
    def _():
        emit(b2[...], b3[...])


def dq_join(where, own, back):
    return pl.pallas_call(
        join_kernel,
        grid_spec=pltpu.PrefetchScalarGridSpec(
            num_scalar_prefetch=1,
            grid=(4,),
            in_specs=[pl.BlockSpec((2, ROWS, WIDTH), lambda i, w: (i % 2, 0, 0))]
            + [pl.BlockSpec((ROWS, WIDTH), lambda i, w: (0, 0))] * HALF,
            out_specs=pl.BlockSpec((TOK, 16, WIDTH), lambda i, w: (0, i, 0)),
        ),
        out_shape=jax.ShapeDtypeStruct((TOK, HEADS, WIDTH), BF16),
        compiler_params=params(),
        name="dq_join",
    )(where, own, *back)


def move(x, count, chips, flip):
    pairs = []
    for i in range(count):
        chip, core = divmod(i, 2)
        pairs.append((i, ((chip + chips) % (count // 2)) * 2 + (core ^ flip)))
    return lax.ppermute(x, "ctx", pairs)


def per_device(queries, keys, values, output, output_cotangent, logsumexp_rows, doc_lengths):
    count = lax.axis_size("ctx")
    where = lax.axis_index("ctx").astype(jnp.int32)[None]
    shift = functools.partial(move, count=count)

    lse = logsumexp_rows.T
    to_sib, same, flip = pack_sib(
        where, queries, output_cotangent, output, lse, keys, values
    )
    sib = shift(to_sib, chips=0, flip=1)
    same1 = shift(same, chips=1, flip=0)
    flip1 = shift(flip, chips=1, flip=1)
    same2 = shift(same, chips=2, flip=0)
    flip2 = shift(flip, chips=2, flip=1)
    own = pack_own(where, queries, output_cotangent, output, lse, same)

    dq, d0s, d0f = phase(0, where, doc_lengths, own, sib)
    r0 = shift(d0f, chips=0, flip=1)
    dq, d1s, d1f = phase(1, where, doc_lengths, own, sib, same1, flip1, dq)
    r1s = shift(d1s, chips=-1, flip=0)
    r1f = shift(d1f, chips=-1, flip=1)
    dq_own, *to_back, d2s, d2f = phase(2, where, doc_lengths, own, sib, same2, flip2, dq)
    d2s, r1s = lax.optimization_barrier((d2s, r1s))
    d2f, r1f = lax.optimization_barrier((d2f, r1f))
    r2s = shift(d2s, chips=-2, flip=0)
    r2f = shift(d2f, chips=-2, flip=1)
    back = [shift(x, chips=0, flip=1) for x in to_back]
    near = near_sum(d0s, r1s, r1f, r0)
    query_grad = dq_join(where, dq_own, back)
    key_grad, value_grad = final_sum(where, near, r2s, r2f)
    return (query_grad, key_grad, value_grad)


def solution(mesh):
    rows = P(("dp", "ctx"), None, None)
    return jax.shard_map(
        per_device,
        mesh=mesh,
        in_specs=(rows,) * 5 + (P(("dp", "ctx"), None), P("dp")),
        out_specs=(rows,) * 3,
        check_vma=False,
    )
```

time: 439 us -> 72.1 us (0.16)
  waiting for transfers between devices: 167 us -> 12.8 us
  matrix products: 126 us -> 0 us
  local copies, waits for them, and re-layouts: 57.6 us -> 1.68 us
  starting transfers between devices: 64.5 us -> 16.2 us
  Pallas kernels: 0 us -> 39.5 us
  other arithmetic: 11.5 us -> 0 us
  loops' own time: 5.62 us -> 0 us
    all_to_all x9 -> x0, waiting for transfers between devices: 167 us -> none  [the longest x1 25.7 us: per_device(): lax.all_to_all(q_grad, 'ctx', split_axis=0, concat_axis=1, tiled=True)]
    dot_general x40 -> x0, matrix products: 126 us -> none  [the longest x8 34.6 us: step(): jnp.einsum('hqk,qhd->kd', prob_b, g_blk, preferred_element_type=jnp.float32)]
    all_to_all x9 -> x0, starting transfers between devices: 64.5 us -> none  [the longest x1 8.27 us: per_device(): lax.all_to_all(key_slots, 'ctx', split_axis=1, concat_axis=0, tiled=True)]
    pallas_call x0 -> x8, Pallas kernels: none -> 39.5 us  [the longest x3 28 us: phase(): pl.pallas_call(functools.partial(phase_kernel, part, heads), grid_spec=pl...]
    unnamed x18 -> x4, local copies, waits for them, and re-layouts: 19.5 us -> 1.68 us
    ppermute x0 -> x14, starting transfers between devices: none -> 16.2 us  [move(): return lax.ppermute(x, 'ctx', pairs)]
    ppermute x0 -> x14, waiting for transfers between devices: none -> 12.8 us  [move(): return lax.ppermute(x, 'ctx', pairs)]
    dynamic_update_slice x16 -> x0, local copies, waits for them, and re-layouts: 7.16 us -> none  [group_grads(): lax.scan(step, (zeros, zeros), jnp.arange(grand_total // block, dtype=jnp...]
  transfers between devices with their start and end apart: 9 -> 14, of which waited for: 8 -> 3; matrix products, arithmetic and copies ran while one was open for 8% -> 0% of each run, Pallas kernels for 0% -> 48%
where the time goes in v2:
time: 72.1 us; the launch traced here: 70.9 us
  Pallas kernels  39.5 us (55%)
  starting transfers between devices  16.2 us (22%)
  waiting for transfers between devices  12.8 us (18%)
  local copies, waits for them, and re-layouts  1.68 us (2%)
    pallas_call x3, Pallas kernels, phase(): pl.pallas_call(functools.partial(phase_kernel, part, heads), grid_spec=pl...  28 us
    ppermute x14, starting transfers between devices, move(): return lax.ppermute(x, 'ctx', pairs)  16.2 us
    ppermute x14, waiting for transfers between devices, move(): return lax.ppermute(x, 'ctx', pairs)  12.8 us
    pallas_call x2, Pallas kernels, pack_call(): pl.pallas_call(kernel, grid_spec=pltpu.PrefetchScalarGridSpec(num_scalar_...  8.3 us
    pallas_call x1, Pallas kernels, dq_join(): pl.pallas_call(join_kernel, grid_spec=pltpu.PrefetchScalarGridSpec(num_sc...  2.01 us
    unnamed x4, local copies, waits for them, and re-layouts  1.68 us
  transfers between devices with their start and end apart: 14, of which 3 were waited for; matrix products, arithmetic and copies ran while one was open for 0% of the time, Pallas kernels for 48%

profile of v2, /device:TPU:55, one launch (start us, length us, event | category | flops | bytes accessed | tf_op | source)
XLA Modules:
  0.0 70.9 jit_solution(16934134327909927392)
XLA Ops:
  0.6 4.4 %pack_sib.1 = (bf16[4,2352,128]{2,1,0:T(8,128)(2,1)}, bf16[2,4,128,128]{3,2,1,0:T(8,128)(2,1)}, bf16[2,4,128,128]{3,2,1,0:T(8,128)(2,1)}) custom-call(s32[1]{0:T(128)} %bitcast.where, bf16[128,64,128]{2,1,0:T(8,128)(2,1)} %q.3, bf16[128,64,128]{2,1,0:T(8,128)(2,1)} %g.3, bf16[128,64,128]{2,1,0:T(8,128)(2,1)} %o.3, f32[64,128]{1,0:T(8,128)} %bitcast.2, ...), custom_call_target="tpu_custom_call" | custom-call | tf_op jit(solution)/shard_map/pack_sib/pallas_call | solution.py:130
  5.0 0.7 collective-permute-start
  5.7 1.5 %collective-permute-start.4 = (bf16[2,4,128,128]{3,2,1,0:T(8,128)(2,1)}, bf16[2,4,128,128]{3,2,1,0:T(8,128)(2,1)S(1)}, u32[]{:S(2)}, u32[]{:S(2)}) collective-permute-start(bf16[2,4,128,128]{3,2,1,0:T(8,128)(2,1)} %get-tuple-element.27), channel_id=1, source_target_pairs={{0,3},{1,2},{2,5},{3,4},{4,7},{5,6},{6,9},{7,8},{8,11},{9,10},{10,... | collective-permute-start | bytes 786440 | tf_op jit(solution)/shard_map/ppermute | solution.py:422
  7.2 0.0 copy-start.1
  7.2 1.2 %collective-permute-start.3 = (bf16[2,4,128,128]{3,2,1,0:T(8,128)(2,1)}, bf16[2,4,128,128]{3,2,1,0:T(8,128)(2,1)S(1)}, u32[]{:S(2)}, u32[]{:S(2)}) collective-permute-start(bf16[2,4,128,128]{3,2,1,0:T(8,128)(2,1)} %get-tuple-element.25.same_ref), channel_id=1, source_target_pairs={{0,2},{1,3},{2,4},{3,5},{4,6},{5,7},{6,8},{7,9},{8,10},{9,11},{10,... | collective-permute-start | bytes 786440 | tf_op jit(solution)/shard_map/ppermute | solution.py:422
  8.4 2.5 %collective-permute-start.2 = (bf16[2,4,128,128]{3,2,1,0:T(8,128)(2,1)}, bf16[2,4,128,128]{3,2,1,0:T(8,128)(2,1)S(1)}, u32[]{:S(2)}, u32[]{:S(2)}) collective-permute-start(bf16[2,4,128,128]{3,2,1,0:T(8,128)(2,1)} %get-tuple-element.27), channel_id=1, source_target_pairs={{0,5},{1,4},{2,7},{3,6},{4,9},{5,8},{6,11},{7,10},{8,13},{9,12},{1... | collective-permute-start | bytes 786440 | tf_op jit(solution)/shard_map/ppermute | solution.py:422
  10.9 2.2 %collective-permute-start.1 = (bf16[2,4,128,128]{3,2,1,0:T(8,128)(2,1)}, bf16[2,4,128,128]{3,2,1,0:T(8,128)(2,1)S(1)}, u32[]{:S(2)}, u32[]{:S(2)}) collective-permute-start(bf16[2,4,128,128]{3,2,1,0:T(8,128)(2,1)} %get-tuple-element.25.same_ref), channel_id=1, source_target_pairs={{0,4},{1,5},{2,6},{3,7},{4,8},{5,9},{6,10},{7,11},{8,12},{9,13},{1... | collective-permute-start | bytes 786440 | tf_op jit(solution)/shard_map/ppermute | solution.py:422
  13.1 3.9 %pack_own.1.refs_0_ = bf16[4,2352,128]{2,1,0:T(8,128)(2,1)} custom-call(s32[1]{0:T(128)} %bitcast.where, bf16[128,64,128]{2,1,0:T(8,128)(2,1)} %q.3, bf16[128,64,128]{2,1,0:T(8,128)(2,1)} %g.3, bf16[128,64,128]{2,1,0:T(8,128)(2,1)} %o.3, f32[64,128]{1,0:T(8,128)} %bitcast.3, bf16[2,4,128,128]{3,2,1,0:T(8,128)(2,1)} %get-tuple-element.25.same_ref), custom_call_target="tpu_custom_call" | custom-call | tf_op jit(solution)/shard_map/pack_own/pallas_call | solution.py:130
  17.0 0.0 collective-permute-done.refs_1_
  17.0 0.0 copy-done.1
  17.0 0.0 copy-start
  17.0 1.7 %copy-done = bf16[4,2352,128]{2,1,0:T(8,128)(2,1)S(1)} copy-done((bf16[4,2352,128]{2,1,0:T(8,128)(2,1)S(1)}, bf16[4,2352,128]{2,1,0:T(8,128)(2,1)}, u32[]{:S(2)}) %copy-start) | copy-done | bytes 2408472
  18.7 9.0 %grads_part0.1 = (f32[2,4,128,1024]{3,2,1,0:T(8,128)}, f32[2,4,128,128]{3,2,1,0:T(8,128)S(1)}, bf16[2,4,128,128]{3,2,1,0:T(8,128)(2,1)S(1)}) custom-call(s32[1]{0:T(128)} %bitcast.where, s32[16]{0:T(128)S(1)} %copy-done.1, bf16[4,2352,128]{2,1,0:T(8,128)(2,1)S(1)} %copy-done, bf16[4,2352,128]{2,1,0:T(8,128)(2,1)} %collective-permute-done.refs_1_), custom_call_target="tpu_custom_call" | custom-call | tf_op jit(solution)/shard_map/grads_part0/pallas_call | solution.py:309
  27.7 0.0 collective-permute-done.4.refs_3_
  27.7 0.0 collective-permute-done.3.refs_2_
  27.7 10.0 %grads_part1.1 = (f32[2,4,128,1024]{3,2,1,0:T(8,128)}, bf16[2,4,128,128]{3,2,1,0:T(8,128)(2,1)S(1)}, bf16[2,4,128,128]{3,2,1,0:T(8,128)(2,1)S(1)}) custom-call(s32[1]{0:T(128)} %bitcast.where, s32[16]{0:T(128)S(1)} %copy-done.1, bf16[4,2352,128]{2,1,0:T(8,128)(2,1)S(1)} %copy-done, bf16[4,2352,128]{2,1,0:T(8,128)(2,1)} %collective-permute-done.refs_1_, ...), custom_call_target="tpu_custom_call" | custom-call | tf_op jit(solution)/shard_map/grads_part1/pallas_call | solution.py:309
  37.7 0.3 collective-permute-start.9
  38.0 0.4 collective-permute-start.10
  38.4 0.0 collective-permute-done.2.refs_3_
  38.4 0.0 collective-permute-done.1.refs_2_
  38.4 9.0 %grads_part2.1 = (bf16[4,1024,128]{2,1,0:T(8,128)(2,1)S(1)}, bf16[1024,128]{1,0:T(8,128)(2,1)S(1)}, bf16[1024,128]{1,0:T(8,128)(2,1)S(1)}, bf16[1024,128]{1,0:T(...) custom-call(s32[1]{0:T(128)} %bitcast.where, ...), custom_call_target="tpu_custom_call" | custom-call | tf_op jit(solution)/shard_map/grads_part2/pallas_call | solution.py:309
  47.4 2.6 %collective-permute-start.5 = (bf16[1024,128]{1,0:T(8,128)(2,1)S(1)}, bf16[1024,128]{1,0:T(8,128)(2,1)S(1)}, u32[]{:S(2)}, u32[]{:S(2)}) collective-permute-start(bf16[1024,128]{1,0:T(8,128)(2,1)S(1)} %get-tuple-element.31), channel_id=1, source_target_pairs={{0,1},{1,0},{2,3},{3,2},{4,5},{5,4},{6,7},{7,6},{8,9},{9,8},{10,11... | collective-permute-start | bytes 786440 | tf_op jit(solution)/shard_map/ppermute | solution.py:422
  49.9 0.1 collective-permute-start.11
  50.0 0.4 collective-permute-start.6
  50.5 0.0 collective-permute-done.9.s1
  50.5 1.2 %collective-permute-start.7 = (bf16[1024,128]{1,0:T(8,128)(2,1)S(1)}, bf16[1024,128]{1,0:T(8,128)(2,1)S(1)}, u32[]{:S(2)}, u32[]{:S(2)}) collective-permute-start(bf16[1024,128]{1,0:T(8,128)(2,1)S(1)} %get-tuple-element.33), channel_id=1, source_target_pairs={{0,1},{1,0},{2,3},{3,2},{4,5},{5,4},{6,7},{7,6},{8,9},{9,8},{10,11... | collective-permute-start | bytes 786440 | tf_op jit(solution)/shard_map/ppermute | solution.py:422
  51.7 2.1 %collective-permute-done.10.f1 = bf16[2,4,128,128]{3,2,1,0:T(8,128)(2,1)S(1)} collective-permute-done((bf16[2,4,128,128]{3,2,1,0:T(8,128)(2,1)S(1)}, bf16[2,4,128,128]{3,2,1,0:T(8,128)(2,1)S(1)}, u32[]{:S(2)}, u32[]{:S(2)}) %collective-permute-start.10) | collective-permute-done | bytes 262176 | tf_op jit(solution)/shard_map/ppermute | solution.py:422
  53.8 0.0 collective-permute-start.8
  53.8 0.0 collective-permute-done.5.b0
  53.8 1.6 %collective-permute-start.12 = (bf16[2,4,128,128]{3,2,1,0:T(8,128)(2,1)S(1)}, bf16[2,4,128,128]{3,2,1,0:T(8,128)(2,1)S(1)}, u32[]{:S(2)}, u32[]{:S(2)}) collective-permute-start(bf16[2,4,128,128]{3,2,1,0:T(8,128)(2,1)S(1)} %get-tuple-element.43), channel_id=1, source_target_pairs={{0,28},{1,29},{2,30},{3,31},{4,0},{5,1},{6,2},{7,3},{8,4},{9,5},{1... | collective-permute-start | bytes 786440 | tf_op jit(solution)/shard_map/ppermute | solution.py:422
  55.4 0.0 collective-permute-done.11.r0
  55.4 1.6 %collective-permute-start.13 = (bf16[2,4,128,128]{3,2,1,0:T(8,128)(2,1)S(1)}, bf16[2,4,128,128]{3,2,1,0:T(8,128)(2,1)S(1)}, u32[]{:S(2)}, u32[]{:S(2)}) collective-permute-start(bf16[2,4,128,128]{3,2,1,0:T(8,128)(2,1)S(1)} %get-tuple-element.44), channel_id=1, source_target_pairs={{0,29},{1,28},{2,31},{3,30},{4,1},{5,0},{6,3},{7,2},{8,5},{9,4},{1... | collective-permute-start | bytes 786440 | tf_op jit(solution)/shard_map/ppermute | solution.py:422
  57.0 0.2 near_sum.1.near
  57.2 0.0 collective-permute-done.6.b1
  57.2 0.0 collective-permute-done.7.b2
  57.2 0.0 collective-permute-done.8.b3
  57.2 2.0 %dq_join.1 = bf16[128,64,128]{2,1,0:T(8,128)(2,1)} custom-call(s32[1]{0:T(128)} %bitcast.where, bf16[4,1024,128]{2,1,0:T(8,128)(2,1)S(1)} %get-tuple-element.30.own, bf16[1024,128]{1,0:T(8,128)(2,1)S(1)} %collective-permute-done.5.b0, bf16[1024,128]{1,0:T(8,128)(2,1)S(1)} %collective-permute-done.6.b1, bf16[1024,128]{1,0:T(8,128)(2,1)S(1)} %collective-permute-done.7.b2, ...), custom_call_target="tpu_custom_call" | custom-call | tf_op jit(solution)/shard_map/dq_join/pallas_call | solution.py:402
  59.2 4.3 %collective-permute-done.12.s2 = bf16[2,4,128,128]{3,2,1,0:T(8,128)(2,1)S(1)} collective-permute-done((bf16[2,4,128,128]{3,2,1,0:T(8,128)(2,1)S(1)}, bf16[2,4,128,128]{3,2,1,0:T(8,128)(2,1)S(1)}, u32[]{:S(2)}, u32[]{:S(2)}) %collective-permute-start.12) | collective-permute-done | bytes 262176 | tf_op jit(solution)/shard_map/ppermute | solution.py:422
  63.6 6.3 %collective-permute-done.13.f2 = bf16[2,4,128,128]{3,2,1,0:T(8,128)(2,1)S(1)} collective-permute-done((bf16[2,4,128,128]{3,2,1,0:T(8,128)(2,1)S(1)}, bf16[2,4,128,128]{3,2,1,0:T(8,128)(2,1)S(1)}, u32[]{:S(2)}, u32[]{:S(2)}) %collective-permute-start.13) | collective-permute-done | bytes 262176 | tf_op jit(solution)/shard_map/ppermute | solution.py:422
  69.9 1.0 %final_sum.1 = (bf16[128,8,128]{2,1,0:T(8,128)(2,1)}, bf16[128,8,128]{2,1,0:T(8,128)(2,1)}) custom-call(s32[1]{0:T(128)} %bitcast.where, f32[2,2,4,128,128]{4,3,2,1,0:T(8,128)S(1)} %near_sum.1.near, bf16[2,4,128,128]{3,2,1,0:T(8,128)(2,1)S(1)} %collective-permute-done.12.s2, bf16[2,4,128,128]{3,2,1,0:T(8,128)(2,1)S(1)} %collective-permute-done.13.f2), custom_call_target="tpu_custom_call" | custom-call | tf_op jit(solution)/shard_map/final_sum/pallas_call | solution.py:361
Async XLA Ops:
  5.0 11.9 %collective-permute-start = (bf16[4,2352,128]{2,1,0:T(8,128)(2,1)}, bf16[4,2352,128]{2,1,0:T(8,128)(2,1)}, u32[]{:S(2)}, u32[]{:S(2)}) collective-permute-start(bf16[4,2352,128]{2,1,0:T(8,128)(2,1)} %get-tuple-element.26), channel_id=1, source_target_pairs={{0,1},{1,0},{2,3},{3,2},{4,5},{5,4},{6,7},{7,6},{8,9},{9,8},{10,11... | collective-permute-start | bytes 7225352 | tf_op jit(solution)/shard_map/ppermute | solution.py:422
  5.7 22.0 %collective-permute-start.4 = (bf16[2,4,128,128]{3,2,1,0:T(8,128)(2,1)}, bf16[2,4,128,128]{3,2,1,0:T(8,128)(2,1)S(1)}, u32[]{:S(2)}, u32[]{:S(2)}) collective-permute-start(bf16[2,4,128,128]{3,2,1,0:T(8,128)(2,1)} %get-tuple-element.27), channel_id=1, source_target_pairs={{0,3},{1,2},{2,5},{3,4},{4,7},{5,6},{6,9},{7,8},{8,11},{9,10},{10,... | collective-permute-start | bytes 786440 | tf_op jit(solution)/shard_map/ppermute | solution.py:422
  7.2 9.8 %copy-start.1 = (s32[16]{0:T(128)S(1)}, s32[16]{0:T(128)}, u32[]{:S(2)}) copy-start(s32[16]{0:T(128)} %lens.5) | copy-start | bytes 196
  7.2 20.5 %collective-permute-start.3 = (bf16[2,4,128,128]{3,2,1,0:T(8,128)(2,1)}, bf16[2,4,128,128]{3,2,1,0:T(8,128)(2,1)S(1)}, u32[]{:S(2)}, u32[]{:S(2)}) collective-permute-start(bf16[2,4,128,128]{3,2,1,0:T(8,128)(2,1)} %get-tuple-element.25.same_ref), channel_id=1, source_target_pairs={{0,2},{1,3},{2,4},{3,5},{4,6},{5,7},{6,8},{7,9},{8,10},{9,11},{10,... | collective-permute-start | bytes 786440 | tf_op jit(solution)/shard_map/ppermute | solution.py:422
  8.4 30.0 %collective-permute-start.2 = (bf16[2,4,128,128]{3,2,1,0:T(8,128)(2,1)}, bf16[2,4,128,128]{3,2,1,0:T(8,128)(2,1)S(1)}, u32[]{:S(2)}, u32[]{:S(2)}) collective-permute-start(bf16[2,4,128,128]{3,2,1,0:T(8,128)(2,1)} %get-tuple-element.27), channel_id=1, source_target_pairs={{0,5},{1,4},{2,7},{3,6},{4,9},{5,8},{6,11},{7,10},{8,13},{9,12},{1... | collective-permute-start | bytes 786440 | tf_op jit(solution)/shard_map/ppermute | solution.py:422
  10.9 27.5 %collective-permute-start.1 = (bf16[2,4,128,128]{3,2,1,0:T(8,128)(2,1)}, bf16[2,4,128,128]{3,2,1,0:T(8,128)(2,1)S(1)}, u32[]{:S(2)}, u32[]{:S(2)}) collective-permute-start(bf16[2,4,128,128]{3,2,1,0:T(8,128)(2,1)} %get-tuple-element.25.same_ref), channel_id=1, source_target_pairs={{0,4},{1,5},{2,6},{3,7},{4,8},{5,9},{6,10},{7,11},{8,12},{9,13},{1... | collective-permute-start | bytes 786440 | tf_op jit(solution)/shard_map/ppermute | solution.py:422
  17.0 1.7 %copy-start = (bf16[4,2352,128]{2,1,0:T(8,128)(2,1)S(1)}, bf16[4,2352,128]{2,1,0:T(8,128)(2,1)}, u32[]{:S(2)}) copy-start(bf16[4,2352,128]{2,1,0:T(8,128)(2,1)} %pack_own.1.refs_0_) | copy-start | bytes 7225348
  37.7 12.7 %collective-permute-start.9 = (bf16[2,4,128,128]{3,2,1,0:T(8,128)(2,1)S(1)}, bf16[2,4,128,128]{3,2,1,0:T(8,128)(2,1)S(1)}, u32[]{:S(2)}, u32[]{:S(2)}) collective-permute-start(bf16[2,4,128,128]{3,2,1,0:T(8,128)(2,1)S(1)} %get-tuple-element.37), channel_id=1, source_target_pairs={{0,30},{1,31},{2,0},{3,1},{4,2},{5,3},{6,4},{7,5},{8,6},{9,7},{10,... | collective-permute-start | bytes 786440 | tf_op jit(solution)/shard_map/ppermute | solution.py:422
  38.0 15.8 %collective-permute-start.10 = (bf16[2,4,128,128]{3,2,1,0:T(8,128)(2,1)S(1)}, bf16[2,4,128,128]{3,2,1,0:T(8,128)(2,1)S(1)}, u32[]{:S(2)}, u32[]{:S(2)}) collective-permute-start(bf16[2,4,128,128]{3,2,1,0:T(8,128)(2,1)S(1)} %get-tuple-element.40), channel_id=1, source_target_pairs={{0,31},{1,30},{2,1},{3,0},{4,3},{5,2},{6,5},{7,4},{8,7},{9,6},{10,... | collective-permute-start | bytes 786440 | tf_op jit(solution)/shard_map/ppermute | solution.py:422
  47.4 6.5 %collective-permute-start.5 = (bf16[1024,128]{1,0:T(8,128)(2,1)S(1)}, bf16[1024,128]{1,0:T(8,128)(2,1)S(1)}, u32[]{:S(2)}, u32[]{:S(2)}) collective-permute-start(bf16[1024,128]{1,0:T(8,128)(2,1)S(1)} %get-tuple-element.31), channel_id=1, source_target_pairs={{0,1},{1,0},{2,3},{3,2},{4,5},{5,4},{6,7},{7,6},{8,9},{9,8},{10,11... | collective-permute-start | bytes 786440 | tf_op jit(solution)/shard_map/ppermute | solution.py:422
  49.9 5.5 %collective-permute-start.11 = (bf16[2,4,128,128]{3,2,1,0:T(8,128)(2,1)S(1)}, bf16[2,4,128,128]{3,2,1,0:T(8,128)(2,1)S(1)}, u32[]{:S(2)}, u32[]{:S(2)}) collective-permute-start(bf16[2,4,128,128]{3,2,1,0:T(8,128)(2,1)S(1)} %get-tuple-element.42), channel_id=1, source_target_pairs={{0,1},{1,0},{2,3},{3,2},{4,5},{5,4},{6,7},{7,6},{8,9},{9,8},{10,11... | collective-permute-start | bytes 786440 | tf_op jit(solution)/shard_map/ppermute | solution.py:422
  50.0 7.2 %collective-permute-start.6 = (bf16[1024,128]{1,0:T(8,128)(2,1)S(1)}, bf16[1024,128]{1,0:T(8,128)(2,1)S(1)}, u32[]{:S(2)}, u32[]{:S(2)}) collective-permute-start(bf16[1024,128]{1,0:T(8,128)(2,1)S(1)} %get-tuple-element.32), channel_id=1, source_target_pairs={{0,1},{1,0},{2,3},{3,2},{4,5},{5,4},{6,7},{7,6},{8,9},{9,8},{10,11... | collective-permute-start | bytes 786440 | tf_op jit(solution)/shard_map/ppermute | solution.py:422
  50.5 6.8 %collective-permute-start.7 = (bf16[1024,128]{1,0:T(8,128)(2,1)S(1)}, bf16[1024,128]{1,0:T(8,128)(2,1)S(1)}, u32[]{:S(2)}, u32[]{:S(2)}) collective-permute-start(bf16[1024,128]{1,0:T(8,128)(2,1)S(1)} %get-tuple-element.33), channel_id=1, source_target_pairs={{0,1},{1,0},{2,3},{3,2},{4,5},{5,4},{6,7},{7,6},{8,9},{9,8},{10,11... | collective-permute-start | bytes 786440 | tf_op jit(solution)/shard_map/ppermute | solution.py:422
  53.8 3.4 %collective-permute-start.8 = (bf16[1024,128]{1,0:T(8,128)(2,1)S(1)}, bf16[1024,128]{1,0:T(8,128)(2,1)S(1)}, u32[]{:S(2)}, u32[]{:S(2)}) collective-permute-start(bf16[1024,128]{1,0:T(8,128)(2,1)S(1)} %get-tuple-element.34), channel_id=1, source_target_pairs={{0,1},{1,0},{2,3},{3,2},{4,5},{5,4},{6,7},{7,6},{8,9},{9,8},{10,11... | collective-permute-start | bytes 786440 | tf_op jit(solution)/shard_map/ppermute | solution.py:422
  53.8 9.8 %collective-permute-start.12 = (bf16[2,4,128,128]{3,2,1,0:T(8,128)(2,1)S(1)}, bf16[2,4,128,128]{3,2,1,0:T(8,128)(2,1)S(1)}, u32[]{:S(2)}, u32[]{:S(2)}) collective-permute-start(bf16[2,4,128,128]{3,2,1,0:T(8,128)(2,1)S(1)} %get-tuple-element.43), channel_id=1, source_target_pairs={{0,28},{1,29},{2,30},{3,31},{4,0},{5,1},{6,2},{7,3},{8,4},{9,5},{1... | collective-permute-start | bytes 786440 | tf_op jit(solution)/shard_map/ppermute | solution.py:422
  55.4 14.4 %collective-permute-start.13 = (bf16[2,4,128,128]{3,2,1,0:T(8,128)(2,1)S(1)}, bf16[2,4,128,128]{3,2,1,0:T(8,128)(2,1)S(1)}, u32[]{:S(2)}, u32[]{:S(2)}) collective-permute-start(bf16[2,4,128,128]{3,2,1,0:T(8,128)(2,1)S(1)} %get-tuple-element.44), channel_id=1, source_target_pairs={{0,29},{1,28},{2,31},{3,30},{4,1},{5,0},{6,3},{7,2},{8,5},{9,4},{1... | collective-permute-start | bytes 786440 | tf_op jit(solution)/shard_map/ppermute | solution.py:422

commit v3 on v2

--- a/solution.py
+++ b/solution.py
@@ -20,7 +20,7 @@
 BF16 = jnp.bfloat16
 VMEM_LIMIT = 48 * 1024 * 1024
 PACK_VMEM = 62 * 1024 * 1024
-PART_VMEM = (VMEM_LIMIT, VMEM_LIMIT, VMEM_LIMIT)
+PART_VMEM = (36 * 1024 * 1024,) * 3
 
 
 def params(limit=VMEM_LIMIT):
@@ -160,7 +160,6 @@
 
 
 RANGES = {0: ((0, 128), (0, 256)), 1: ((0, 256), (0, 256)), 2: ((0, 256), (128, 256))}
-CHUNK = 1024
 
 
 def positions(chip, s):
@@ -177,122 +176,127 @@
     return low
 
 
-def grads(part, chip, s, k, v, q, g, lse, delta, low, first, emit_dq):
-    size = k.shape[0]
+def products(k, v, q, g):
+    return dot(k, q, 1, 1), dot(v, g, 1, 1)
+
+
+def weights(part, chip, s, first, score, dprob, lse, delta, low):
     base = (chip - part) * 2 * TOK + first
-    dk = dv = None
-    at = positions(chip, s) if part == 0 else None
-    for r in range(0, ROWS, CHUNK):
-        cols = slice(r, r + CHUNK)
-        qc = q[cols]
-        gc = g[cols]
-        j = base + lax.broadcasted_iota(jnp.int32, (size, CHUNK), 0)
-        visible = j >= low[:, cols]
-        if part == 0:
-            visible = visible & (j <= at[:, cols])
-        score = dot(k, qc, 1, 1)
-        prob = jnp.where(visible, jnp.exp2(score * (SCALE * LOG2E) - lse[:, cols]), 0.0)
-        dvc = dot(prob.astype(BF16), gc, 1, 0)
-        dprob = dot(v, gc, 1, 1)
-        ds = (prob * (dprob - delta[:, cols])).astype(BF16)
-        dkc = dot(ds, qc, 1, 0)
-        dk = dkc if dk is None else dk + dkc
-        dv = dvc if dv is None else dv + dvc
-        emit_dq(cols, dot(k, ds, 0, 0))
-    return dk * SCALE, dv
-
-
-def phase_kernel(part, heads, where, lens, *refs):
-    own, sib = refs[:2]
-    qg_s, st_s, kv_s, acc_s, dq_s = refs[-5:]
+    j = base + lax.broadcasted_iota(jnp.int32, score.shape, 0)
+    visible = j >= low
+    if part == 0:
+        visible = visible & (j <= positions(chip, s))
+    prob = jnp.where(visible, jnp.exp2(score * (SCALE * LOG2E) - lse), 0.0)
+    return prob.astype(BF16), (prob * (dprob - delta)).astype(BF16)
+
+
+def phase_kernel(part, where, lens, *refs):
     index = where[0]
     core = index % 2
     chip = index // 2
     own_at = pl.ds(pl.multiple_of(core * TOK, TOK), TOK)
     sib_at = pl.ds(pl.multiple_of((1 - core) * TOK, TOK), TOK)
-    for half, src in ((core, own), (1 - core, sib)):
-        qg_s[half] = src[:, : 2 * ROWS, :]
-        for i in range(heads):
-            st = src[i, 2 * ROWS + 2 * TOK :, :].astype(F32)
-            st_s[half, i, 0:1] = unfold(st[0:8] + st[8:16] + st[16:24]) * LOG2E
-            st_s[half, i, 1:2] = unfold(st[24:32] + st[32:40] + st[40:48])
+    copies = []
     if part == 0:
-        dq_out, d_same, d_flip = refs[2:5]
-        for half, src in ((own_at, own), (sib_at, sib)):
-            kv_s[0, :, half, :] = src[:, 2 * ROWS : 2 * ROWS + TOK, :]
-            kv_s[1, :, half, :] = src[:, 2 * ROWS + TOK : 2 * ROWS + 2 * TOK, :]
+        own, sib, rows_s, dq_out, d_same, d_flip, st_s, acc_s, dq_s, sems = refs
+        for i in range(HALF):
+            for n, (half, src) in enumerate(((core, own), (1 - core, sib))):
+                copy = pltpu.make_async_copy(src.at[i], rows_s.at[half, i], sems.at[n, i])
+                copy.start()
+                copies.append(copy)
+    elif part == 1:
+        rows_s, dq_in, same, flip, dq_out, d_same, d_flip, st_s, kv_s, acc_s, dq_s = refs
     else:
-        same, flip, dq_in = refs[2:5]
+        rows_s, dq_in, same, flip, dq_own, *back = refs[:9]
+        d_same, d_flip, st_s, kv_s, acc_s, dq_s = refs[9:]
+    if part != 0:
         kv_s[:, :, own_at, :] = same[...]
         kv_s[:, :, sib_at, :] = flip[...]
-        if part == 1:
-            dq_out, d_same, d_flip = refs[5:8]
-        else:
-            dq_own, *back, d_same, d_flip = refs[5:12]
+
+    def stats(i, s):
+        st = rows_s[s, i, 2 * ROWS + 2 * TOK :, :].astype(F32)
+        st_s[s, i, 0:1] = unfold(st[0:8] + st[8:16] + st[16:24]) * LOG2E
+        st_s[s, i, 1:2] = unfold(st[24:32] + st[32:40] + st[40:48])
+
     if part != 1:
         acc_s[...] = jnp.zeros_like(acc_s)
-
-    for s in range(2):
-        low = doc_starts(lens, positions(chip, s))
-        for i in range(heads):
-            first, last = RANGES[part][s]
-
-            def emit(cols, d):
-                if part == 0:
-                    dq_out[s, i, :, cols] = d
-                elif part == 1:
-                    dq_out[s, i, :, cols] = dq_in[s, i, :, cols] + d
-                else:
-                    full = jnp.transpose(dq_in[s, i, :, cols] + d) * SCALE
-                    dq_s[s, i, cols, :] = full.astype(BF16)
-
-            dk, dv = grads(
-                part,
-                chip,
-                s,
-                kv_s[0, i, first:last, :],
-                kv_s[1, i, first:last, :],
-                qg_s[s, i, :ROWS],
-                qg_s[s, i, ROWS:],
-                st_s[s, i, 0:1],
-                st_s[s, i, 1:2],
-                low,
-                first,
-                emit,
-            )
-            fresh = part == 1 and s == 0
-            acc_s[0, i, first:last, :] = dk if fresh else acc_s[0, i, first:last, :] + dk
-            acc_s[1, i, first:last, :] = dv if fresh else acc_s[1, i, first:last, :] + dv
+    lows = [doc_starts(lens, positions(chip, s)) for s in range(2)]
+    items = [(i, s) for i in range(HALF) for s in range(2)]
+
+    def key_rows(which, i, s):
+        first, last = RANGES[part][s]
+        if part != 0:
+            return kv_s[which, i, first:last, :]
+        at = slice(2 * ROWS + which * TOK, 2 * ROWS + (which + 1) * TOK)
+        if s == 0:
+            return rows_s[0, i, at, :]
+        return jnp.concatenate([rows_s[0, i, at, :], rows_s[1, i, at, :]], axis=0)
+
+    def start(i, s):
+        if part == 0 and s == 0:
+            for copy in copies[2 * i : 2 * i + 2]:
+                copy.wait()
+        stats(i, s)
+        return products(
+            key_rows(0, i, s), key_rows(1, i, s), rows_s[s, i, :ROWS], rows_s[s, i, ROWS : 2 * ROWS]
+        )
+
+    ahead = start(*items[0])
+    for n, (i, s) in enumerate(items):
+        first, last = RANGES[part][s]
+        score, dprob = ahead
+        if n + 1 < len(items):
+            ahead = start(*items[n + 1])
+        prob, ds = weights(
+            part, chip, s, first, score, dprob, st_s[s, i, 0:1], st_s[s, i, 1:2], lows[s]
+        )
+        dv = dot(prob, rows_s[s, i, ROWS : 2 * ROWS], 1, 0)
+        dk = dot(ds, rows_s[s, i, :ROWS], 1, 0) * SCALE
+        fresh = part == 1 and s == 0
+        acc_s[0, i, first:last, :] = dk if fresh else acc_s[0, i, first:last, :] + dk
+        acc_s[1, i, first:last, :] = dv if fresh else acc_s[1, i, first:last, :] + dv
+        d = dot(key_rows(0, i, s), ds, 0, 0)
+        if part == 0:
+            dq_out[s, i] = d
+        elif part == 1:
+            dq_out[s, i] = dq_in[s, i] + d
+        else:
+            dq_s[s, i] = (jnp.transpose(dq_in[s, i] + d) * SCALE).astype(BF16)
 
     d_same[...] = acc_s[:, :, own_at, :].astype(d_same.dtype)
     d_flip[...] = acc_s[:, :, sib_at, :].astype(d_flip.dtype)
     if part == 2:
         dq_own[...] = dq_s[core]
-        for n in range(HALF // heads):
-
-            @pl.when(pl.program_id(0) == n)
-            def _():
-                for i in range(heads):
-                    back[n * heads + i][...] = dq_s[1 - core, i]
-
-
-def phase(part, where, lens, own, sib, same=None, flip=None, dq=None, heads=2):
-    pack_spec = pl.BlockSpec((heads, PACK, WIDTH), lambda i, w, l: (i, 0, 0))
-    kv_spec = pl.BlockSpec((2, heads, TOK, WIDTH), lambda i, w, l: (0, i, 0, 0))
-    dq_spec = pl.BlockSpec((2, heads, WIDTH, ROWS), lambda i, w, l: (0, i, 0, 0))
+        for i in range(HALF):
+            back[i][...] = dq_s[1 - core, i]
+
+
+def phase(part, where, lens, rows, same=None, flip=None, dq=None):
+    vmem = pl.BlockSpec(memory_space=pltpu.VMEM)
+    hbm = pl.BlockSpec(memory_space=pltpu.HBM)
+    kv_spec = pl.BlockSpec((2, HALF, TOK, WIDTH), lambda i, w, l: (0, 0, 0, 0))
+    rows_shape = jax.ShapeDtypeStruct((2, HALF, PACK, WIDTH), BF16)
     dq_shape = jax.ShapeDtypeStruct((2, HALF, WIDTH, ROWS), F32)
     kv_shape = jax.ShapeDtypeStruct((2, HALF, TOK, WIDTH), BF16)
-    args = [own, sib]
-    in_specs = [pack_spec, pack_spec]
+    scratch = [pltpu.VMEM((2, HALF, 2, ROWS), F32)]
+    if part != 0:
+        scratch.append(pltpu.VMEM((2, HALF, 2 * TOK, WIDTH), BF16))
+    scratch += [
+        pltpu.VMEM((2, HALF, 2 * TOK, WIDTH), F32),
+        pltpu.VMEM((2, HALF, ROWS, WIDTH) if part == 2 else (8, WIDTH), BF16),
+    ]
     if part == 0:
-        out_shape = [dq_shape, jax.ShapeDtypeStruct((2, HALF, TOK, WIDTH), F32), kv_shape]
-        out_specs = [dq_spec, kv_spec, kv_spec]
+        args = rows
+        in_specs = [hbm, hbm]
+        out_shape = [rows_shape, dq_shape, jax.ShapeDtypeStruct((2, HALF, TOK, WIDTH), F32), kv_shape]
+        out_specs = [vmem, vmem, kv_spec, kv_spec]
+        scratch.append(pltpu.SemaphoreType.DMA((2, HALF)))
     else:
-        args += [same, flip, dq]
-        in_specs += [kv_spec, kv_spec, dq_spec]
+        args = (rows, dq, same, flip)
+        in_specs = [vmem, vmem, kv_spec, kv_spec]
         if part == 1:
             out_shape = [dq_shape, kv_shape, kv_shape]
-            out_specs = [dq_spec, kv_spec, kv_spec]
+            out_specs = [vmem, kv_spec, kv_spec]
         else:
             out_shape = [
                 jax.ShapeDtypeStruct((HALF, ROWS, WIDTH), BF16),
@@ -301,25 +305,19 @@
                 kv_shape,
             ]
             out_specs = [
-                pl.BlockSpec((heads, ROWS, WIDTH), lambda i, w, l: (i, 0, 0)),
+                pl.BlockSpec((HALF, ROWS, WIDTH), lambda i, w, l: (0, 0, 0)),
                 *[pl.BlockSpec((ROWS, WIDTH), lambda i, w, l: (0, 0))] * HALF,
                 kv_spec,
                 kv_spec,
             ]
     return pl.pallas_call(
-        functools.partial(phase_kernel, part, heads),
+        functools.partial(phase_kernel, part),
         grid_spec=pltpu.PrefetchScalarGridSpec(
             num_scalar_prefetch=2,
-            grid=(HALF // heads,),
+            grid=(1,),
             in_specs=in_specs,
             out_specs=out_specs,
-            scratch_shapes=[
-                pltpu.VMEM((2, heads, 2 * ROWS, WIDTH), BF16),
-                pltpu.VMEM((2, heads, 2, ROWS), F32),
-                pltpu.VMEM((2, heads, 2 * TOK, WIDTH), BF16),
-                pltpu.VMEM((2, heads, 2 * TOK, WIDTH), F32),
-                pltpu.VMEM((2, heads, ROWS, WIDTH), BF16),
-            ],
+            scratch_shapes=scratch,
         ),
         out_shape=out_shape,
         compiler_params=params(PART_VMEM[part]),
@@ -434,18 +432,20 @@
     sib = shift(to_sib, chips=0, flip=1)
     same1 = shift(same, chips=1, flip=0)
     flip1 = shift(flip, chips=1, flip=1)
-    same2 = shift(same, chips=2, flip=0)
-    flip2 = shift(flip, chips=2, flip=1)
     own = pack_own(where, queries, output_cotangent, output, lse, same)
 
-    dq, d0s, d0f = phase(0, where, doc_lengths, own, sib)
+    far_same, far_flip, own = lax.optimization_barrier((same, flip, own))
+    same2 = shift(far_same, chips=2, flip=0)
+    flip2 = shift(far_flip, chips=2, flip=1)
+    rows, dq, d0s, d0f = phase(0, where, doc_lengths, (own, sib))
     r0 = shift(d0f, chips=0, flip=1)
-    dq, d1s, d1f = phase(1, where, doc_lengths, own, sib, same1, flip1, dq)
+    dq, d1s, d1f = phase(1, where, doc_lengths, rows, same1, flip1, dq)
     r1s = shift(d1s, chips=-1, flip=0)
     r1f = shift(d1f, chips=-1, flip=1)
-    dq_own, *to_back, d2s, d2f = phase(2, where, doc_lengths, own, sib, same2, flip2, dq)
-    d2s, r1s = lax.optimization_barrier((d2s, r1s))
-    d2f, r1f = lax.optimization_barrier((d2f, r1f))
+    dq, r0 = lax.optimization_barrier((dq, r0))
+    dq_own, *to_back, d2s, d2f = phase(2, where, doc_lengths, rows, same2, flip2, dq)
+    to_back[2], r1s = lax.optimization_barrier((to_back[2], r1s))
+    to_back[3], r1f = lax.optimization_barrier((to_back[3], r1f))
     r2s = shift(d2s, chips=-2, flip=0)
     r2f = shift(d2f, chips=-2, flip=1)
     back = [shift(x, chips=0, flip=1) for x in to_back]

time: 72.1 us -> 65.9 us (0.914)
  the two profiles are of different devices: /device:TPU:55 before, /device:TPU:110 now
where the time goes in v3:
time: 65.9 us; the launch traced here: 65.7 us
  Pallas kernels  31.4 us (48%)
  waiting for transfers between devices  21.5 us (33%)
  starting transfers between devices  10.4 us (16%)
  local copies, waits for them, and re-layouts  1.69 us (3%)
  between operations  0.7 us (1%)
    ppermute x14, waiting for transfers between devices, move(): return lax.ppermute(x, 'ctx', pairs)  21.5 us
    pallas_call x3, Pallas kernels, phase(): pl.pallas_call(functools.partial(phase_kernel, part), grid_spec=pltpu.Pre...  19.9 us
    ppermute x14, starting transfers between devices, move(): return lax.ppermute(x, 'ctx', pairs)  10.4 us
    pallas_call x2, Pallas kernels, pack_call(): pl.pallas_call(kernel, grid_spec=pltpu.PrefetchScalarGridSpec(num_scalar_...  8.34 us
    pallas_call x1, Pallas kernels, dq_join(): pl.pallas_call(join_kernel, grid_spec=pltpu.PrefetchScalarGridSpec(num_sc...  2 us
    unnamed x8, local copies, waits for them, and re-layouts  1.69 us
  transfers between devices with their start and end apart: 14, of which 4 were waited for; matrix products, arithmetic and copies ran while one was open for 0% of the time, Pallas kernels for 38%

profile of v3, /device:TPU:110, one launch (start us, length us, event | category | flops | bytes accessed | tf_op | source)
XLA Modules:
  0.0 65.7 jit_solution(16734137286510187860)
XLA Ops:
  0.6 4.4 %pack_sib.1 = (bf16[4,2352,128]{2,1,0:T(8,128)(2,1)}, bf16[2,4,128,128]{3,2,1,0:T(8,128)(2,1)}, bf16[2,4,128,128]{3,2,1,0:T(8,128)(2,1)}) custom-call(s32[1]{0:T(128)} %bitcast.where, bf16[128,64,128]{2,1,0:T(8,128)(2,1)} %q.3, bf16[128,64,128]{2,1,0:T(8,128)(2,1)} %g.3, bf16[128,64,128]{2,1,0:T(8,128)(2,1)} %o.3, f32[64,128]{1,0:T(8,128)} %bitcast.2, ...), custom_call_target="tpu_custom_call" | custom-call | tf_op jit(solution)/shard_map/pack_sib/pallas_call | solution.py:130
  5.1 0.0 collective-permute-start
  5.1 0.1 collective-permute-start.1
  5.1 0.0 copy-start.1
  5.2 0.3 collective-permute-start.2
  5.5 3.9 %pack_own.1.refs_0_ = bf16[4,2352,128]{2,1,0:T(8,128)(2,1)} custom-call(s32[1]{0:T(128)} %bitcast.where, bf16[128,64,128]{2,1,0:T(8,128)(2,1)} %q.3, bf16[128,64,128]{2,1,0:T(8,128)(2,1)} %g.3, bf16[128,64,128]{2,1,0:T(8,128)(2,1)} %o.3, f32[64,128]{1,0:T(8,128)} %bitcast.3, bf16[2,4,128,128]{3,2,1,0:T(8,128)(2,1)} %get-tuple-element.40.same_ref), custom_call_target="tpu_custom_call" | custom-call | tf_op jit(solution)/shard_map/pack_own/pallas_call | solution.py:130
  9.4 0.6 collective-permute-done.refs_1_
  10.0 0.0 copy-done.1
  10.0 0.0 copy-start
  10.0 1.7 %copy-done = bf16[4,2352,128]{2,1,0:T(8,128)(2,1)S(1)} copy-done((bf16[4,2352,128]{2,1,0:T(8,128)(2,1)S(1)}, bf16[4,2352,128]{2,1,0:T(8,128)(2,1)}, u32[]{:S(2)}) %copy-start) | copy-done | bytes 2408472
  11.7 0.0 copy-start.2
  11.7 0.0 copy-start.3
  11.7 7.4 %grads_part0.1 = (bf16[2,4,2352,128]{3,2,1,0:T(8,128)(2,1)S(1)}, f32[2,4,128,1024]{3,2,1,0:T(8,128)S(1)}, f32[2,4,128,128]{3,2,1,0:T(8,128)S(1)}, bf16[2,4,128,128]{3,2,1,0:T(8,128)(2,1)S(1)}) custom-call(s32[1]{0:T(128)} %bitcast.where, s32[16]{0:T(128)S(1)} %copy-done.1, bf16[4,2352,128]{2,1,0:T(8,128)(2,1)S(1)} %copy-done, ...), custom_call_target="tpu_custom_call" | custom-call | tf_op jit(solution)/shard_map/grads_part0/pallas_call | solution.py:313
  19.1 0.2 collective-permute-start.3
  19.3 0.0 copy-done.2
  19.3 1.7 %collective-permute-start.4 = (bf16[2,4,128,128]{3,2,1,0:T(8,128)(2,1)S(1)}, bf16[2,4,128,128]{3,2,1,0:T(8,128)(2,1)S(1)}, u32[]{:S(2)}, u32[]{:S(2)}) collective-permute-start(bf16[2,4,128,128]{3,2,1,0:T(8,128)(2,1)S(1)} %copy-done.2), channel_id=1, source_target_pairs={{0,4},{1,5},{2,6},{3,7},{4,8},{5,9},{6,10},{7,11},{8,12},{9,13},{1... | collective-permute-start | bytes 786440 | tf_op jit(solution)/shard_map/ppermute | solution.py:420
  21.0 0.0 copy-done.3
  21.0 2.2 %collective-permute-start.5 = (bf16[2,4,128,128]{3,2,1,0:T(8,128)(2,1)S(1)}, bf16[2,4,128,128]{3,2,1,0:T(8,128)(2,1)S(1)}, u32[]{:S(2)}, u32[]{:S(2)}) collective-permute-start(bf16[2,4,128,128]{3,2,1,0:T(8,128)(2,1)S(1)} %copy-done.3), channel_id=1, source_target_pairs={{0,5},{1,4},{2,7},{3,6},{4,9},{5,8},{6,11},{7,10},{8,13},{9,12},{1... | collective-permute-start | bytes 786440 | tf_op jit(solution)/shard_map/ppermute | solution.py:420
  23.3 0.0 collective-permute-done.1.refs_2_
  23.3 0.0 collective-permute-done.2.refs_3_
  23.3 6.6 %grads_part1.1 = (f32[2,4,128,1024]{3,2,1,0:T(8,128)S(1)}, bf16[2,4,128,128]{3,2,1,0:T(8,128)(2,1)S(1)}, bf16[2,4,128,128]{3,2,1,0:T(8,128)(2,1)S(1)}) custom-call(s32[1]{0:T(128)} %bitcast.where, s32[16]{0:T(128)S(1)} %copy-done.1, bf16[2,4,2352,128]{3,2,1,0:T(8,128)(2,1)S(1)} %get-tuple-element.35.refs_0_, ...), custom_call_target="tpu_custom_call" | custom-call | tf_op jit(solution)/shard_map/grads_part1/pallas_call | solution.py:313
  29.9 0.8 %collective-permute-start.10 = (bf16[2,4,128,128]{3,2,1,0:T(8,128)(2,1)S(1)}, bf16[2,4,128,128]{3,2,1,0:T(8,128)(2,1)S(1)}, u32[]{:S(2)}, u32[]{:S(2)}) collective-permute-start(bf16[2,4,128,128]{3,2,1,0:T(8,128)(2,1)S(1)} %get-tuple-element.49), channel_id=1, source_target_pairs={{0,31},{1,30},{2,1},{3,0},{4,3},{5,2},{6,5},{7,4},{8,7},{9,6},{10,... | collective-permute-start | bytes 786440 | tf_op jit(solution)/shard_map/ppermute | solution.py:420
  30.8 0.2 collective-permute-start.8
  31.0 0.0 collective-permute-done.3.r0
  31.0 0.0 collective-permute-done.4.refs_2_
  31.0 3.5 %collective-permute-done.5.refs_3_ = bf16[2,4,128,128]{3,2,1,0:T(8,128)(2,1)S(1)} collective-permute-done((bf16[2,4,128,128]{3,2,1,0:T(8,128)(2,1)S(1)}, bf16[2,4,128,128]{3,2,1,0:T(8,128)(2,1)S(1)}, u32[]{:S(2)}, u32[]{:S(2)}) %collective-permute-start.5) | collective-permute-done | bytes 262176 | tf_op jit(solution)/shard_map/ppermute | solution.py:420
  34.5 5.9 %grads_part2.1 = (bf16[4,1024,128]{2,1,0:T(8,128)(2,1)S(1)}, bf16[1024,128]{1,0:T(8,128)(2,1)S(1)}, bf16[1024,128]{1,0:T(8,128)(2,1)S(1)}, bf16[1024,128]{1,0:T(...) custom-call(s32[1]{0:T(128)} %bitcast.where, ...), custom_call_target="tpu_custom_call" | custom-call | tf_op jit(solution)/shard_map/grads_part2/pallas_call | solution.py:313
  40.3 3.7 %collective-permute-start.12 = (bf16[2,4,128,128]{3,2,1,0:T(8,128)(2,1)S(1)}, bf16[2,4,128,128]{3,2,1,0:T(8,128)(2,1)S(1)}, u32[]{:S(2)}, u32[]{:S(2)}) collective-permute-start(bf16[2,4,128,128]{3,2,1,0:T(8,128)(2,1)S(1)} %get-tuple-element.55), channel_id=1, source_target_pairs={{0,28},{1,29},{2,30},{3,31},{4,0},{5,1},{6,2},{7,3},{8,4},{9,5},{1... | collective-permute-start | bytes 786440 | tf_op jit(solution)/shard_map/ppermute | solution.py:420
  44.0 0.0 collective-permute-done.10.f1
  44.0 9.3 %collective-permute-done.8.s1 = bf16[2,4,128,128]{3,2,1,0:T(8,128)(2,1)S(1)} collective-permute-done((bf16[2,4,128,128]{3,2,1,0:T(8,128)(2,1)S(1)}, bf16[2,4,128,128]{3,2,1,0:T(8,128)(2,1)S(1)}, u32[]{:S(2)}, u32[]{:S(2)}) %collective-permute-start.8) | collective-permute-done | bytes 262176 | tf_op jit(solution)/shard_map/ppermute | solution.py:420
  53.3 0.0 collective-permute-start.13
  53.3 0.0 collective-permute-start.11
  53.3 0.5 collective-permute-start.9
  53.8 0.0 collective-permute-start.6
  53.8 0.0 collective-permute-done.12.s2
  53.8 0.5 collective-permute-start.7
  54.3 0.2 near_sum.1.near
  54.5 8.2 %collective-permute-done.13.f2 = bf16[2,4,128,128]{3,2,1,0:T(8,128)(2,1)S(1)} collective-permute-done((bf16[2,4,128,128]{3,2,1,0:T(8,128)(2,1)S(1)}, bf16[2,4,128,128]{3,2,1,0:T(8,128)(2,1)S(1)}, u32[]{:S(2)}, u32[]{:S(2)}) %collective-permute-start.13) | collective-permute-done | bytes 262176 | tf_op jit(solution)/shard_map/ppermute | solution.py:420
  62.7 1.0 %final_sum.1 = (bf16[128,8,128]{2,1,0:T(8,128)(2,1)}, bf16[128,8,128]{2,1,0:T(8,128)(2,1)}) custom-call(s32[1]{0:T(128)} %bitcast.where, f32[2,2,4,128,128]{4,3,2,1,0:T(8,128)S(1)} %near_sum.1.near, bf16[2,4,128,128]{3,2,1,0:T(8,128)(2,1)S(1)} %collective-permute-done.12.s2, bf16[2,4,128,128]{3,2,1,0:T(8,128)(2,1)S(1)} %collective-permute-done.13.f2), custom_call_target="tpu_custom_call" | custom-call | tf_op jit(solution)/shard_map/final_sum/pallas_call | solution.py:359
  63.7 0.0 collective-permute-done.11.b3
  63.7 0.0 collective-permute-done.9.b2
  63.7 0.0 collective-permute-done.6.b0
  63.7 0.0 collective-permute-done.7.b1
  63.7 2.0 %dq_join.1 = bf16[128,64,128]{2,1,0:T(8,128)(2,1)} custom-call(s32[1]{0:T(128)} %bitcast.where, bf16[4,1024,128]{2,1,0:T(8,128)(2,1)S(1)} %get-tuple-element.42.own, bf16[1024,128]{1,0:T(8,128)(2,1)S(1)} %collective-permute-done.6.b0, bf16[1024,128]{1,0:T(8,128)(2,1)S(1)} %collective-permute-done.7.b1, bf16[1024,128]{1,0:T(8,128)(2,1)S(1)} %collective-permute-done.9.b2, ...), custom_call_target="tpu_custom_call" | custom-call | tf_op jit(solution)/shard_map/dq_join/pallas_call | solution.py:400
Async XLA Ops:
  5.1 4.9 %collective-permute-start = (bf16[4,2352,128]{2,1,0:T(8,128)(2,1)}, bf16[4,2352,128]{2,1,0:T(8,128)(2,1)}, u32[]{:S(2)}, u32[]{:S(2)}) collective-permute-start(bf16[4,2352,128]{2,1,0:T(8,128)(2,1)} %get-tuple-element.34), channel_id=1, source_target_pairs={{0,1},{1,0},{2,3},{3,2},{4,5},{5,4},{6,7},{7,6},{8,9},{9,8},{10,11... | collective-permute-start | bytes 7225352 | tf_op jit(solution)/shard_map/ppermute | solution.py:420
  5.1 18.2 %collective-permute-start.1 = (bf16[2,4,128,128]{3,2,1,0:T(8,128)(2,1)}, bf16[2,4,128,128]{3,2,1,0:T(8,128)(2,1)S(1)}, u32[]{:S(2)}, u32[]{:S(2)}) collective-permute-start(bf16[2,4,128,128]{3,2,1,0:T(8,128)(2,1)} %get-tuple-element.40.same_ref), channel_id=1, source_target_pairs={{0,2},{1,3},{2,4},{3,5},{4,6},{5,7},{6,8},{7,9},{8,10},{9,11},{10,... | collective-permute-start | bytes 786440 | tf_op jit(solution)/shard_map/ppermute | solution.py:420
  5.1 4.9 %copy-start.1 = (s32[16]{0:T(128)S(1)}, s32[16]{0:T(128)}, u32[]{:S(2)}) copy-start(s32[16]{0:T(128)} %lens.5) | copy-start | bytes 196
  5.2 18.1 %collective-permute-start.2 = (bf16[2,4,128,128]{3,2,1,0:T(8,128)(2,1)}, bf16[2,4,128,128]{3,2,1,0:T(8,128)(2,1)S(1)}, u32[]{:S(2)}, u32[]{:S(2)}) collective-permute-start(bf16[2,4,128,128]{3,2,1,0:T(8,128)(2,1)} %get-tuple-element.41), channel_id=1, source_target_pairs={{0,3},{1,2},{2,5},{3,4},{4,7},{5,6},{6,9},{7,8},{8,11},{9,10},{10,... | collective-permute-start | bytes 786440 | tf_op jit(solution)/shard_map/ppermute | solution.py:420
  10.0 1.7 %copy-start = (bf16[4,2352,128]{2,1,0:T(8,128)(2,1)S(1)}, bf16[4,2352,128]{2,1,0:T(8,128)(2,1)}, u32[]{:S(2)}) copy-start(bf16[4,2352,128]{2,1,0:T(8,128)(2,1)} %pack_own.1.refs_0_) | copy-start | bytes 7225348
  11.7 7.6 %copy-start.2 = (bf16[2,4,128,128]{3,2,1,0:T(8,128)(2,1)S(1)}, bf16[2,4,128,128]{3,2,1,0:T(8,128)(2,1)}, u32[]{:S(2)}) copy-start(bf16[2,4,128,128]{3,2,1,0:T(8,128)(2,1)} %get-tuple-element.40.same_ref) | copy-start | bytes 786436
  11.7 9.3 %copy-start.3 = (bf16[2,4,128,128]{3,2,1,0:T(8,128)(2,1)S(1)}, bf16[2,4,128,128]{3,2,1,0:T(8,128)(2,1)}, u32[]{:S(2)}) copy-start(bf16[2,4,128,128]{3,2,1,0:T(8,128)(2,1)} %get-tuple-element.41) | copy-start | bytes 786436
  19.1 11.9 %collective-permute-start.3 = (bf16[2,4,128,128]{3,2,1,0:T(8,128)(2,1)S(1)}, bf16[2,4,128,128]{3,2,1,0:T(8,128)(2,1)S(1)}, u32[]{:S(2)}, u32[]{:S(2)}) collective-permute-start(bf16[2,4,128,128]{3,2,1,0:T(8,128)(2,1)S(1)} %get-tuple-element.38), channel_id=1, source_target_pairs={{0,1},{1,0},{2,3},{3,2},{4,5},{5,4},{6,7},{7,6},{8,9},{9,8},{10,11... | collective-permute-start | bytes 786440 | tf_op jit(solution)/shard_map/ppermute | solution.py:420
  19.3 11.7 %collective-permute-start.4 = (bf16[2,4,128,128]{3,2,1,0:T(8,128)(2,1)S(1)}, bf16[2,4,128,128]{3,2,1,0:T(8,128)(2,1)S(1)}, u32[]{:S(2)}, u32[]{:S(2)}) collective-permute-start(bf16[2,4,128,128]{3,2,1,0:T(8,128)(2,1)S(1)} %copy-done.2), channel_id=1, source_target_pairs={{0,4},{1,5},{2,6},{3,7},{4,8},{5,9},{6,10},{7,11},{8,12},{9,13},{1... | collective-permute-start | bytes 786440 | tf_op jit(solution)/shard_map/ppermute | solution.py:420
  21.0 13.4 %collective-permute-start.5 = (bf16[2,4,128,128]{3,2,1,0:T(8,128)(2,1)S(1)}, bf16[2,4,128,128]{3,2,1,0:T(8,128)(2,1)S(1)}, u32[]{:S(2)}, u32[]{:S(2)}) collective-permute-start(bf16[2,4,128,128]{3,2,1,0:T(8,128)(2,1)S(1)} %copy-done.3), channel_id=1, source_target_pairs={{0,5},{1,4},{2,7},{3,6},{4,9},{5,8},{6,11},{7,10},{8,13},{9,12},{1... | collective-permute-start | bytes 786440 | tf_op jit(solution)/shard_map/ppermute | solution.py:420
  29.9 14.1 %collective-permute-start.10 = (bf16[2,4,128,128]{3,2,1,0:T(8,128)(2,1)S(1)}, bf16[2,4,128,128]{3,2,1,0:T(8,128)(2,1)S(1)}, u32[]{:S(2)}, u32[]{:S(2)}) collective-permute-start(bf16[2,4,128,128]{3,2,1,0:T(8,128)(2,1)S(1)} %get-tuple-element.49), channel_id=1, source_target_pairs={{0,31},{1,30},{2,1},{3,0},{4,3},{5,2},{6,5},{7,4},{8,7},{9,6},{10,... | collective-permute-start | bytes 786440 | tf_op jit(solution)/shard_map/ppermute | solution.py:420
  30.8 22.5 %collective-permute-start.8 = (bf16[2,4,128,128]{3,2,1,0:T(8,128)(2,1)S(1)}, bf16[2,4,128,128]{3,2,1,0:T(8,128)(2,1)S(1)}, u32[]{:S(2)}, u32[]{:S(2)}) collective-permute-start(bf16[2,4,128,128]{3,2,1,0:T(8,128)(2,1)S(1)} %get-tuple-element.46), channel_id=1, source_target_pairs={{0,30},{1,31},{2,0},{3,1},{4,2},{5,3},{6,4},{7,5},{8,6},{9,7},{10,... | collective-permute-start | bytes 786440 | tf_op jit(solution)/shard_map/ppermute | solution.py:420
  40.3 13.5 %collective-permute-start.12 = (bf16[2,4,128,128]{3,2,1,0:T(8,128)(2,1)S(1)}, bf16[2,4,128,128]{3,2,1,0:T(8,128)(2,1)S(1)}, u32[]{:S(2)}, u32[]{:S(2)}) collective-permute-start(bf16[2,4,128,128]{3,2,1,0:T(8,128)(2,1)S(1)} %get-tuple-element.55), channel_id=1, source_target_pairs={{0,28},{1,29},{2,30},{3,31},{4,0},{5,1},{6,2},{7,3},{8,4},{9,5},{1... | collective-permute-start | bytes 786440 | tf_op jit(solution)/shard_map/ppermute | solution.py:420
  53.3 9.4 %collective-permute-start.13 = (bf16[2,4,128,128]{3,2,1,0:T(8,128)(2,1)S(1)}, bf16[2,4,128,128]{3,2,1,0:T(8,128)(2,1)S(1)}, u32[]{:S(2)}, u32[]{:S(2)}) collective-permute-start(bf16[2,4,128,128]{3,2,1,0:T(8,128)(2,1)S(1)} %get-tuple-element.56), channel_id=1, source_target_pairs={{0,29},{1,28},{2,31},{3,30},{4,1},{5,0},{6,3},{7,2},{8,5},{9,4},{1... | collective-permute-start | bytes 786440 | tf_op jit(solution)/shard_map/ppermute | solution.py:420
  53.3 10.4 %collective-permute-start.11 = (bf16[1024,128]{1,0:T(8,128)(2,1)S(1)}, bf16[1024,128]{1,0:T(8,128)(2,1)S(1)}, u32[]{:S(2)}, u32[]{:S(2)}) collective-permute-start(bf16[1024,128]{1,0:T(8,128)(2,1)S(1)} %get-tuple-element.50), channel_id=1, source_target_pairs={{0,1},{1,0},{2,3},{3,2},{4,5},{5,4},{6,7},{7,6},{8,9},{9,8},{10,11... | collective-permute-start | bytes 786440 | tf_op jit(solution)/shard_map/ppermute | solution.py:420
  53.3 10.4 %collective-permute-start.9 = (bf16[1024,128]{1,0:T(8,128)(2,1)S(1)}, bf16[1024,128]{1,0:T(8,128)(2,1)S(1)}, u32[]{:S(2)}, u32[]{:S(2)}) collective-permute-start(bf16[1024,128]{1,0:T(8,128)(2,1)S(1)} %get-tuple-element.47), channel_id=1, source_target_pairs={{0,1},{1,0},{2,3},{3,2},{4,5},{5,4},{6,7},{7,6},{8,9},{9,8},{10,11... | collective-permute-start | bytes 786440 | tf_op jit(solution)/shard_map/ppermute | solution.py:420
  53.8 9.9 %collective-permute-start.6 = (bf16[1024,128]{1,0:T(8,128)(2,1)S(1)}, bf16[1024,128]{1,0:T(8,128)(2,1)S(1)}, u32[]{:S(2)}, u32[]{:S(2)}) collective-permute-start(bf16[1024,128]{1,0:T(8,128)(2,1)S(1)} %get-tuple-element.43), channel_id=1, source_target_pairs={{0,1},{1,0},{2,3},{3,2},{4,5},{5,4},{6,7},{7,6},{8,9},{9,8},{10,11... | collective-permute-start | bytes 786440 | tf_op jit(solution)/shard_map/ppermute | solution.py:420
  53.8 9.9 %collective-permute-start.7 = (bf16[1024,128]{1,0:T(8,128)(2,1)S(1)}, bf16[1024,128]{1,0:T(8,128)(2,1)S(1)}, u32[]{:S(2)}, u32[]{:S(2)}) collective-permute-start(bf16[1024,128]{1,0:T(8,128)(2,1)S(1)} %get-tuple-element.44), channel_id=1, source_target_pairs={{0,1},{1,0},{2,3},{3,2},{4,5},{5,4},{6,7},{7,6},{8,9},{9,8},{10,11... | collective-permute-start | bytes 786440 | tf_op jit(solution)/shard_map/ppermute | solution.py:420
